TPU v7x, 128 devices: a whole 4x4x4 slice. The times are simulated.
128 devices in a mesh: wide: 16 (over z_lo, x, core), narrow: 8 (over z_hi, y).
Axes of the slice: x: 4, y: 4, z: 4 (z_hi: 2, z_lo: 2; z = z_hi * 2 + z_lo), core: 2. Of those that a mesh axis runs over, the one named last changes fastest.
Arguments:
- velocity: float32 [3, 128, 64, 128], P(None, 'wide', 'narrow'), may hold values from -6 to 6
- force: float32 [3, 128, 64, 128], P(None, 'wide', 'narrow'), may hold values from -6 to 6
- visc_class: int32 [128, 64, 128], P('wide', 'narrow'), may hold values from 0 to 3
- visc_table: float32 [4], replicated, may hold values from 0.2 to 5
- multiplier: float32 [3, 256, 2048], P(None, ('wide', 'narrow')), may hold values from -6 to 6
- marker_cell: int32 [256, 2048], P(('wide', 'narrow')), may hold values from 0 to 8190, as said below
- marker_frac: float32 [3, 256, 2048], P(None, ('wide', 'narrow')), may hold values from 0 to 1
- pair_sphere: int32 [4096], P(('wide', 'narrow')), may hold values from 0 to 1
- pair_partner: int32 [4096], P(('wide', 'narrow')), may hold values from 0 to 17
- pair_normal: float32 [3, 4096], P(None, ('wide', 'narrow')), may hold values from -6 to 6
- pair_gap: float32 [4096], P(('wide', 'narrow')), may hold values from -6 to 6
- contact_force: float32 [4096], P(('wide', 'narrow')), may hold values from 0 to 1
Outputs:
- fluid_velocity: float32 [3, 128, 64, 128], P(None, 'wide', 'narrow')
- rigid_multiplier: float32 [3, 256, 2048], P(None, ('wide', 'narrow'))
- contact_multiplier: float32 [4096], P(('wide', 'narrow'))
Inputs may be any that keep to these rules, and one draw needn't show every extreme that they name: marker_cell[s, m] = (i * 8 + j) * 128 + k for a cell (i, j, k) of the brick that owns sphere s, with k <= 126; the markers of one sphere lie within a few cells of each other.
All inputs are finite; a program needn't handle non-finite values.
Results may differ from a plain program's by a relative error of at most 0.0003.
Values sent between devices are 32-bit elements; how exact they have to be, the bound alone decides.
A program may use at most 64 MiB of HBM per device.

v0:
```python
import jax
import jax.numpy as jnp
from jax import lax
from jax.sharding import PartitionSpec as P

ITERS = 2
SWEEPS = 2


base_diag = 1.0
spread_gain = 0.25
rigid_step = 0.5
contact_step = 0.5
contact_gain = 0.5


def extended(array, sides, width):
    for axis, dim in sides:
        devices, length = (lax.axis_size(axis), array.shape[dim])
        up = [(i, (i + 1) % devices) for i in range(devices - 1)]
        down = [(j, i) for i, j in up]
        last = lax.slice_in_dim(array, length - width, length, axis=dim)
        first = lax.slice_in_dim(array, 0, width, axis=dim)
        before = lax.ppermute(last, axis, up)
        after = lax.ppermute(first, axis, down)
        array = jnp.concatenate([before, array, after], axis=dim)
    return array


def passed_along(array, axis, by):
    devices = lax.axis_size(axis)
    pairs = [(i, i + by) for i in range(devices) if 0 <= i + by < devices]
    return lax.ppermute(array, axis, pairs)


def separable_weights(marker_cell, marker_frac, cells_y, depth, span_x, span_y, lift):
    cell_x = (marker_cell // (cells_y * depth)).reshape(-1)
    cell_y = (marker_cell // depth % cells_y).reshape(-1)
    cell_z = (marker_cell % depth).reshape(-1)
    frac = marker_frac.reshape(3, -1)
    plane_ids = jnp.arange(span_x * span_y, dtype=jnp.int32)
    plane_weight = jnp.zeros((cell_x.shape[0], span_x * span_y), jnp.float32)
    for step_x in (0, 1):
        for step_y in (0, 1):
            corner_index = (cell_x + lift + step_x) * span_y + cell_y + lift + step_y
            weight_x = frac[0] if step_x else 1.0 - frac[0]
            weight_y = frac[1] if step_y else 1.0 - frac[1]
            plane_weight = plane_weight + jnp.where(
                corner_index[:, None] == plane_ids[None, :],
                (weight_x * weight_y)[:, None],
                jnp.float32(0.0),
            )
    depth_ids = jnp.arange(depth, dtype=jnp.int32)
    depth_weight = jnp.where(
        cell_z[:, None] == depth_ids[None, :], (1.0 - frac[2])[:, None], jnp.float32(0.0)
    ) + jnp.where(cell_z[:, None] + 1 == depth_ids[None, :], frac[2][:, None], jnp.float32(0.0))
    return (plane_weight, depth_weight)


def extend(field):
    return extended(field, (("wide", 1), ("narrow", 2)), 1)


def partners(sphere_vel, pair_partner):
    comps, spheres = sphere_vel.shape
    grown = extended(sphere_vel[None, None], (("wide", 0), ("narrow", 1)), 1)
    table = jnp.transpose(grown, (2, 0, 1, 3)).reshape(comps, 9 * spheres)
    picker = (pair_partner[None, :] == jnp.arange(9 * spheres, dtype=jnp.int32)[:, None]).astype(
        jnp.float32
    )
    return jnp.dot(table, picker, precision=lax.Precision.HIGHEST)


def local(
    velocity,
    force,
    visc_class,
    visc_table,
    multiplier,
    marker_cell,
    marker_frac,
    pair_sphere,
    pair_partner,
    pair_normal,
    pair_gap,
    contact_force,
):
    comps, cells_x, cells_y, depth = velocity.shape
    spheres, markers = marker_cell.shape
    classes = jnp.arange(visc_table.shape[0], dtype=jnp.int32)
    viscosity = jnp.sum(
        jnp.where(
            visc_class[None] == classes[:, None, None, None],
            visc_table[:, None, None, None],
            jnp.float32(0.0),
        ),
        axis=0,
    )
    visc_grown = extended(viscosity, (("wide", 0), ("narrow", 1)), 1)
    visc_grown = jnp.pad(visc_grown, ((0, 0), (0, 0), (1, 1)))
    face_coef = [
        0.5 * (viscosity + visc_grown[:-2, 1:-1, 1:-1]),
        0.5 * (viscosity + visc_grown[2:, 1:-1, 1:-1]),
        0.5 * (viscosity + visc_grown[1:-1, :-2, 1:-1]),
        0.5 * (viscosity + visc_grown[1:-1, 2:, 1:-1]),
        0.5 * (viscosity + visc_grown[1:-1, 1:-1, :-2]),
        0.5 * (viscosity + visc_grown[1:-1, 1:-1, 2:]),
    ]
    diagonal = (
        base_diag
        + face_coef[0]
        + face_coef[1]
        + face_coef[2]
        + face_coef[3]
        + face_coef[4]
        + face_coef[5]
    )
    read_plane, read_depth = separable_weights(
        marker_cell, marker_frac, cells_y, depth, cells_x + 2, cells_y + 2, 1
    )
    write_plane, write_depth = separable_weights(
        marker_cell, marker_frac, cells_y, depth, cells_x + 1, cells_y + 1, 0
    )
    owner_onehot = (pair_sphere[None, :] == jnp.arange(spheres, dtype=jnp.int32)[:, None]).astype(
        jnp.float32
    )
    for outer in range(ITERS):
        flat_mult = multiplier.reshape(comps, -1)
        spread_list = []
        for comp in range(comps):
            scaled = (spread_gain * flat_mult[comp])[:, None] * write_depth
            spread_list.append(jnp.dot(write_plane.T, scaled, precision=lax.Precision.HIGHEST))
        grid = jnp.stack(spread_list).reshape(comps, cells_x + 1, cells_y + 1, depth)
        arrived = passed_along(grid[:, cells_x], "wide", 1)
        grid = grid[:, :cells_x].at[:, 0].add(arrived)
        arrived = passed_along(grid[:, :, cells_y], "narrow", 1)
        grid = grid[:, :, :cells_y].at[:, :, 0].add(arrived)
        rhs = force + grid
        for inner in range(SWEEPS):
            grown = jnp.pad(extend(velocity), ((0, 0), (0, 0), (0, 0), (1, 1)))
            neighbour_sum = (
                face_coef[0] * grown[:, :-2, 1:-1, 1:-1]
                + face_coef[1] * grown[:, 2:, 1:-1, 1:-1]
                + face_coef[2] * grown[:, 1:-1, :-2, 1:-1]
                + face_coef[3] * grown[:, 1:-1, 2:, 1:-1]
                + face_coef[4] * grown[:, 1:-1, 1:-1, :-2]
                + face_coef[5] * grown[:, 1:-1, 1:-1, 2:]
            )
            velocity = (rhs + neighbour_sum) / diagonal
        plane_vel = extend(velocity).reshape(comps, (cells_x + 2) * (cells_y + 2), depth)
        sample_list = []
        for comp in range(comps):
            nearby = jnp.dot(read_plane, plane_vel[comp], precision=lax.Precision.HIGHEST)
            sample_list.append(jnp.sum(nearby * read_depth, axis=1))
        marker_vel = jnp.stack(sample_list).reshape(comps, spheres, markers)
        push = jnp.dot(
            pair_normal * contact_force[None], owner_onehot.T, precision=lax.Precision.HIGHEST
        )
        sphere_vel = jnp.mean(marker_vel, axis=2) + contact_gain * push
        multiplier = multiplier + rigid_step * (sphere_vel[:, :, None] - marker_vel)
        own_vel = jnp.dot(sphere_vel, owner_onehot, precision=lax.Precision.HIGHEST)
        partner_vel = partners(sphere_vel, pair_partner)
        closing = jnp.sum(pair_normal * (partner_vel - own_vel), axis=0)
        contact_force = jnp.maximum(
            jnp.float32(0.0), contact_force - contact_step * (pair_gap + closing)
        )
    return (velocity, multiplier, contact_force)


def solution(mesh):
    in_specs = (
        P(None, "wide", "narrow", None),
        P(None, "wide", "narrow", None),
        P("wide", "narrow", None),
        P(),
        P(None, ("wide", "narrow"), None),
        P(("wide", "narrow"), None),
        P(None, ("wide", "narrow"), None),
        P(("wide", "narrow")),
        P(("wide", "narrow")),
        P(None, ("wide", "narrow")),
        P(("wide", "narrow")),
        P(("wide", "narrow")),
    )
    out_specs = (
        P(None, "wide", "narrow", None),
        P(None, ("wide", "narrow"), None),
        P(("wide", "narrow")),
    )
    return jax.shard_map(local, mesh=mesh, in_specs=in_specs, out_specs=out_specs, check_vma=False)
```

profile of v0, /device:TPU:96, one launch (start us, length us, event | category | flops | bytes accessed | tf_op | source)
XLA Modules:
  0.0 323.8 jit_solution(17102358346485707409)
XLA Ops:
  1.4 3.9 %collective-permute-start.5 = (f32[3,1,8,128]{3,2,1,0:T(8,128)S(1)}, f32[3,1,8,128]{3,2,1,0:T(8,128)S(1)}, u32[]{:S(2)}, u32[]{:S(2)}) collective-permute-start(f32[3,1,8,128]{3,2,1,0:T(8,128)S(1)} %get-tuple-element.95), channel_id=1, source_target_pairs={{8,0},{16,8},{24,16},{32,24},{40,32},{48,40},{56,48},{64,56},{72,6... | collective-permute-start | bytes 36872 | tf_op jit(solution)/shard_map/ppermute | solution.py:25
  8.1 5.8 %collective-permute-start.4 = (f32[1,8,128]{2,1,0:T(8,128)S(1)}, f32[1,8,128]{2,1,0:T(8,128)S(1)}, u32[]{:S(2)}, u32[]{:S(2)}) collective-permute-start(f32[1,8,128]{2,1,0:T(8,128)S(1)} %get-tuple-element.117), channel_id=1, source_target_pairs={{8,0},{16,8},{24,16},{32,24},{40,32},{48,40},{56,48},{64,56},{72,6... | collective-permute-start | bytes 12296 | tf_op jit(solution)/shard_map/ppermute | solution.py:25
  17.7 12.2 %fusion.8 = f32[81,128]{1,0:T(8,128)S(1)} fusion(f32[4096]{0:T(1024)S(1)} %bitcast.167, f32[4096]{0:T(1024)S(1)} %bitcast.124, s32[4096]{0:T(1024)S(1)} %get-tuple-element.121, f32[4096]{0:T(1024)S(1)} %get-tuple-element.120, s32[4096]{0:T(1024)S(1)} %bitcast.104, f32[4096]{0:T(1024)S(1)} %get-tuple-element.115, s32[4096]{0:T(1024)S(1)} %get-tuple-element.122, ...), kind=kOutput, calls=%fused_computation.14 | convolution fusion | flops 516403200 | bytes 254464 | tf_op jit(solution)/shard_map/dot_general | solution.py:132
  29.8 12.2 %fusion.6 = f32[81,128]{1,0:T(8,128)S(1)} fusion(f32[4096]{0:T(1024)S(1)} %bitcast.165, f32[4096]{0:T(1024)S(1)} %bitcast.125, s32[4096]{0:T(1024)S(1)} %get-tuple-element.121, f32[4096]{0:T(1024)S(1)} %get-tuple-element.120, s32[4096]{0:T(1024)S(1)} %bitcast.105, f32[4096]{0:T(1024)S(1)} %get-tuple-element.115, s32[4096]{0:T(1024)S(1)} %get-tuple-element.122, ...), kind=kOutput, calls=%fused_computation.12 | convolution fusion | flops 516403200 | bytes 254464 | tf_op jit(solution)/shard_map/dot_general | solution.py:132
  42.0 12.2 %fusion.10 = f32[81,128]{1,0:T(8,128)S(1)} fusion(f32[4096]{0:T(1024)S(1)} %bitcast.126, s32[4096]{0:T(1024)S(1)} %get-tuple-element.121, f32[4096]{0:T(1024)S(1)} %get-tuple-element.120, s32[4096]{0:T(1024)S(1)} %bitcast.106, f32[4096]{0:T(1024)S(1)} %bitcast.166, f32[4096]{0:T(1024)S(1)} %get-tuple-element.115, s32[4096]{0:T(1024)S(1)} %get-tuple-element.122, ...), kind=kOutput, calls=%fused_computation.16 | convolution fusion | flops 516403200 | bytes 254464 | tf_op jit(solution)/shard_map/dot_general | solution.py:132
  54.3 4.6 %collective-permute-start.8 = (f32[10,1,128]{2,1,0:T(1,128)S(1)}, f32[10,1,128]{2,1,0:T(1,128)S(1)}, u32[]{:S(2)}, u32[]{:S(2)}) collective-permute-start(f32[10,1,128]{2,1,0:T(1,128)S(1)} %get-tuple-element.106), channel_id=1, source_target_pairs={{1,0},{2,1},{3,2},{4,3},{5,4},{6,5},{7,6},{9,8},{10,9},{11,10},{12... | collective-permute-start | bytes 15368 | tf_op jit(solution)/shard_map/ppermute | solution.py:25
  62.9 5.1 %collective-permute-done.6 = f32[10,1,128]{2,1,0:T(1,128)S(1)} collective-permute-done((f32[10,1,128]{2,1,0:T(1,128)S(1)}, f32[10,1,128]{2,1,0:T(1,128)S(1)}, u32[]{:S(2)}, u32[]{:S(2)}) %collective-permute-start.6) | collective-permute-done | bytes 5152 | tf_op jit(solution)/shard_map/ppermute | solution.py:24
  71.2 3.5 %collective-permute-start.7 = (f32[3,10,1,128]{3,2,1,0:T(1,128)S(1)}, f32[3,10,1,128]{3,2,1,0:T(1,128)S(1)}, u32[]{:S(2)}, u32[]{:S(2)}) collective-permute-start(f32[3,10,1,128]{3,2,1,0:T(1,128)S(1)} %get-tuple-element.83), channel_id=1, source_target_pairs={{0,1},{1,2},{2,3},{3,4},{4,5},{5,6},{6,7},{8,9},{9,10},{10,11},{11... | collective-permute-start | bytes 46088 | tf_op jit(solution)/shard_map/ppermute | solution.py:24
  74.7 6.0 %collective-permute-start.9 = (f32[3,10,1,128]{3,2,1,0:T(1,128)S(1)}, f32[3,10,1,128]{3,2,1,0:T(1,128)S(1)}, u32[]{:S(2)}, u32[]{:S(2)}) collective-permute-start(f32[3,10,1,128]{3,2,1,0:T(1,128)S(1)} %get-tuple-element.84), channel_id=1, source_target_pairs={{1,0},{2,1},{3,2},{4,3},{5,4},{6,5},{7,6},{9,8},{10,9},{11,10},{12... | collective-permute-start | bytes 46088 | tf_op jit(solution)/shard_map/ppermute | solution.py:25
  84.5 5.8 %collective-permute-start.11 = (f32[3,1,8,128]{3,2,1,0:T(8,128)S(1)}, f32[3,1,8,128]{3,2,1,0:T(8,128)S(1)}, u32[]{:S(2)}, u32[]{:S(2)}) collective-permute-start(f32[3,1,8,128]{3,2,1,0:T(8,128)S(1)} %get-tuple-element.94), channel_id=1, source_target_pairs={{8,0},{16,8},{24,16},{32,24},{40,32},{48,40},{56,48},{64,56},{72,6... | collective-permute-start | bytes 36872 | tf_op jit(solution)/shard_map/ppermute | solution.py:25
  93.6 7.8 %collective-permute-start.13 = (f32[3,10,1,128]{3,2,1,0:T(1,128)S(1)}, f32[3,10,1,128]{3,2,1,0:T(1,128)S(1)}, u32[]{:S(2)}, u32[]{:S(2)}) collective-permute-start(f32[3,10,1,128]{3,2,1,0:T(1,128)S(1)} %get-tuple-element.82), channel_id=1, source_target_pairs={{1,0},{2,1},{3,2},{4,3},{5,4},{6,5},{7,6},{9,8},{10,9},{11,10},{12... | collective-permute-start | bytes 46088 | tf_op jit(solution)/shard_map/ppermute | solution.py:25
  105.3 5.8 %collective-permute-start.15 = (f32[3,1,8,128]{3,2,1,0:T(8,128)S(1)}, f32[3,1,8,128]{3,2,1,0:T(8,128)S(1)}, u32[]{:S(2)}, u32[]{:S(2)}) collective-permute-start(f32[3,1,8,128]{3,2,1,0:T(8,128)S(1)} %get-tuple-element.92), channel_id=1, source_target_pairs={{8,0},{16,8},{24,16},{32,24},{40,32},{48,40},{56,48},{64,56},{72,6... | collective-permute-start | bytes 36872 | tf_op jit(solution)/shard_map/ppermute | solution.py:25
  114.4 7.8 %collective-permute-start.17 = (f32[3,10,1,128]{3,2,1,0:T(1,128)S(1)}, f32[3,10,1,128]{3,2,1,0:T(1,128)S(1)}, u32[]{:S(2)}, u32[]{:S(2)}) collective-permute-start(f32[3,10,1,128]{3,2,1,0:T(1,128)S(1)} %get-tuple-element.80), channel_id=1, source_target_pairs={{1,0},{2,1},{3,2},{4,3},{5,4},{6,5},{7,6},{9,8},{10,9},{11,10},{12... | collective-permute-start | bytes 46088 | tf_op jit(solution)/shard_map/ppermute | solution.py:25
  123.7 11.5 %fusion.14 = f32[4096]{0:T(1024)S(1)} fusion(f32[100,128]{1,0:T(8,128)S(1)} %squeeze.33, f32[4096]{0:T(1024)S(1)} %bitcast.127, s32[4096]{0:T(1024)S(1)} %get-tuple-element.121, f32[4096]{0:T(1024)S(1)} %get-tuple-element.120, s32[4096]{0:T(1024)S(1)} %bitcast.107, f32[4096]{0:T(1024)S(1)} %get-tuple-element.115, s32[4096]{0:T(1024)S(1)} %bitcast.159, ...), kind=kOutput, calls=%fused_computation.33 | convolution fusion | flops 637317120 | bytes 264192 | tf_op jit(solution)/shard_map/dot_general | solution.py:153
  135.3 11.5 %fusion.13 = f32[4096]{0:T(1024)S(1)} fusion(f32[100,128]{1,0:T(8,128)S(1)} %squeeze.32, f32[4096]{0:T(1024)S(1)} %bitcast.128, s32[4096]{0:T(1024)S(1)} %get-tuple-element.121, f32[4096]{0:T(1024)S(1)} %get-tuple-element.120, s32[4096]{0:T(1024)S(1)} %bitcast.108, f32[4096]{0:T(1024)S(1)} %get-tuple-element.115, s32[4096]{0:T(1024)S(1)} %bitcast.160, ...), kind=kOutput, calls=%fused_computation.32 | convolution fusion | flops 637317120 | bytes 264192 | tf_op jit(solution)/shard_map/dot_general | solution.py:153
  146.9 11.5 %fusion.12 = f32[4096]{0:T(1024)S(1)} fusion(f32[100,128]{1,0:T(8,128)S(1)} %squeeze.31, f32[4096]{0:T(1024)S(1)} %bitcast.129, s32[4096]{0:T(1024)S(1)} %get-tuple-element.121, f32[4096]{0:T(1024)S(1)} %get-tuple-element.120, s32[4096]{0:T(1024)S(1)} %bitcast.109, f32[4096]{0:T(1024)S(1)} %get-tuple-element.115, s32[4096]{0:T(1024)S(1)} %bitcast.161, ...), kind=kOutput, calls=%fused_computation.31 | convolution fusion | flops 637317120 | bytes 264192 | tf_op jit(solution)/shard_map/dot_general | solution.py:153
  159.1 12.1 %fusion.2 = f32[81,128]{1,0:T(8,128)S(1)} fusion(f32[4096]{0:T(1024)S(1)} %bitcast.170, f32[4096]{0:T(1024)S(1)} %bitcast.130, s32[4096]{0:T(1024)S(1)} %get-tuple-element.121, f32[4096]{0:T(1024)S(1)} %get-tuple-element.120, s32[4096]{0:T(1024)S(1)} %bitcast.110, f32[4096]{0:T(1024)S(1)} %get-tuple-element.115, s32[4096]{0:T(1024)S(1)} %get-tuple-element.122, ...), kind=kOutput, calls=%fused_computation.8 | convolution fusion | flops 516403200 | bytes 254464 | tf_op jit(solution)/shard_map/dot_general | solution.py:132
  171.3 12.1 %fusion = f32[81,128]{1,0:T(8,128)S(1)} fusion(f32[4096]{0:T(1024)S(1)} %bitcast.169, f32[4096]{0:T(1024)S(1)} %bitcast.131, s32[4096]{0:T(1024)S(1)} %get-tuple-element.121, f32[4096]{0:T(1024)S(1)} %get-tuple-element.120, s32[4096]{0:T(1024)S(1)} %bitcast.111, f32[4096]{0:T(1024)S(1)} %get-tuple-element.115, s32[4096]{0:T(1024)S(1)} %get-tuple-element.122, ...), kind=kOutput, calls=%fused_computation.6 | convolution fusion | flops 516403200 | bytes 254464 | tf_op jit(solution)/shard_map/dot_general | solution.py:132
  183.5 12.2 %fusion.4 = f32[81,128]{1,0:T(8,128)S(1)} fusion(f32[4096]{0:T(1024)S(1)} %bitcast.168, f32[4096]{0:T(1024)S(1)} %bitcast.132, s32[4096]{0:T(1024)S(1)} %get-tuple-element.121, f32[4096]{0:T(1024)S(1)} %get-tuple-element.120, s32[4096]{0:T(1024)S(1)} %bitcast.112, f32[4096]{0:T(1024)S(1)} %get-tuple-element.115, s32[4096]{0:T(1024)S(1)} %get-tuple-element.122, ...), kind=kOutput, calls=%fused_computation.10 | convolution fusion | flops 516403200 | bytes 254464 | tf_op jit(solution)/shard_map/dot_general | solution.py:132
  197.9 5.1 %collective-permute-done.18 = f32[3,9,128]{2,0,1:T(4,128)S(1)} collective-permute-done((f32[3,9,128]{2,0,1:T(4,128)S(1)}, f32[3,9,128]{2,0,1:T(4,128)S(1)}, u32[]{:S(2)}, u32[]{:S(2)}) %collective-permute-start.18) | collective-permute-done | bytes 13856 | tf_op jit(solution)/shard_map/ppermute | solution.py:33
  214.7 5.8 %collective-permute-start.21 = (f32[3,1,8,128]{3,2,1,0:T(8,128)S(1)}, f32[3,1,8,128]{3,2,1,0:T(8,128)S(1)}, u32[]{:S(2)}, u32[]{:S(2)}) collective-permute-start(f32[3,1,8,128]{3,2,1,0:T(8,128)S(1)} %get-tuple-element.90), channel_id=1, source_target_pairs={{8,0},{16,8},{24,16},{32,24},{40,32},{48,40},{56,48},{64,56},{72,6... | collective-permute-start | bytes 36872 | tf_op jit(solution)/shard_map/ppermute | solution.py:25
  220.5 4.8 %collective-permute-start.31 = (f32[3,1,3,2]{2,3,1,0:T(2,128)S(1)}, f32[3,1,3,2]{2,3,1,0:T(2,128)S(1)}, u32[]{:S(2)}, u32[]{:S(2)}) collective-permute-start(f32[3,1,3,2]{2,3,1,0:T(2,128)S(1)} %pad_maximum_fusion.55), channel_id=1, source_target_pairs={{1,0},{2,1},{3,2},{4,3},{5,4},{6,5},{7,6},{9,8},{10,9},{11,10},{12... | collective-permute-start | bytes 224 | tf_op jit(solution)/shard_map/ppermute | solution.py:25
  229.3 7.5 %collective-permute-start.23 = (f32[3,10,1,128]{3,2,1,0:T(1,128)S(1)}, f32[3,10,1,128]{3,2,1,0:T(1,128)S(1)}, u32[]{:S(2)}, u32[]{:S(2)}) collective-permute-start(f32[3,10,1,128]{3,2,1,0:T(1,128)S(1)} %get-tuple-element.78), channel_id=1, source_target_pairs={{1,0},{2,1},{3,2},{4,3},{5,4},{6,5},{7,6},{9,8},{10,9},{11,10},{12... | collective-permute-start | bytes 46088 | tf_op jit(solution)/shard_map/ppermute | solution.py:25
  240.7 5.8 %collective-permute-start.25 = (f32[3,1,8,128]{3,2,1,0:T(8,128)S(1)}, f32[3,1,8,128]{3,2,1,0:T(8,128)S(1)}, u32[]{:S(2)}, u32[]{:S(2)}) collective-permute-start(f32[3,1,8,128]{3,2,1,0:T(8,128)S(1)} %get-tuple-element.88), channel_id=1, source_target_pairs={{8,0},{16,8},{24,16},{32,24},{40,32},{48,40},{56,48},{64,56},{72,6... | collective-permute-start | bytes 36872 | tf_op jit(solution)/shard_map/ppermute | solution.py:25
  249.8 8.0 %collective-permute-start.27 = (f32[3,10,1,128]{3,2,1,0:T(1,128)S(1)}, f32[3,10,1,128]{3,2,1,0:T(1,128)S(1)}, u32[]{:S(2)}, u32[]{:S(2)}) collective-permute-start(f32[3,10,1,128]{3,2,1,0:T(1,128)S(1)} %get-tuple-element.76), channel_id=1, source_target_pairs={{1,0},{2,1},{3,2},{4,3},{5,4},{6,5},{7,6},{9,8},{10,9},{11,10},{12... | collective-permute-start | bytes 46088 | tf_op jit(solution)/shard_map/ppermute | solution.py:25
  259.1 11.5 %fusion.17 = f32[4096]{0:T(1024)S(1)} fusion(f32[100,128]{1,0:T(8,128)S(1)} %squeeze.72, f32[4096]{0:T(1024)S(1)} %bitcast.133, s32[4096]{0:T(1024)S(1)} %get-tuple-element.121, f32[4096]{0:T(1024)S(1)} %get-tuple-element.120, s32[4096]{0:T(1024)S(1)} %bitcast.113, f32[4096]{0:T(1024)S(1)} %get-tuple-element.115, s32[4096]{0:T(1024)S(1)} %bitcast.162, ...), kind=kOutput, calls=%fused_computation.36 | convolution fusion | flops 637317120 | bytes 264192 | tf_op jit(solution)/shard_map/dot_general | solution.py:153
  270.7 11.5 %fusion.16 = f32[4096]{0:T(1024)S(1)} fusion(f32[100,128]{1,0:T(8,128)S(1)} %squeeze.71, f32[4096]{0:T(1024)S(1)} %bitcast.134, s32[4096]{0:T(1024)S(1)} %get-tuple-element.121, f32[4096]{0:T(1024)S(1)} %get-tuple-element.120, s32[4096]{0:T(1024)S(1)} %bitcast.114, f32[4096]{0:T(1024)S(1)} %get-tuple-element.115, s32[4096]{0:T(1024)S(1)} %bitcast.163, ...), kind=kOutput, calls=%fused_computation.35 | convolution fusion | flops 637317120 | bytes 264192 | tf_op jit(solution)/shard_map/dot_general | solution.py:153
  282.3 11.5 %fusion.15 = f32[4096]{0:T(1024)S(1)} fusion(f32[100,128]{1,0:T(8,128)S(1)} %squeeze.70, f32[4096]{0:T(1024)S(1)} %bitcast.135, s32[4096]{0:T(1024)S(1)} %get-tuple-element.121, f32[4096]{0:T(1024)S(1)} %get-tuple-element.120, s32[4096]{0:T(1024)S(1)} %bitcast.115, f32[4096]{0:T(1024)S(1)} %get-tuple-element.115, s32[4096]{0:T(1024)S(1)} %bitcast.164, ...), kind=kOutput, calls=%fused_computation.34 | convolution fusion | flops 637317120 | bytes 264192 | tf_op jit(solution)/shard_map/dot_general | solution.py:153
  294.5 4.3 %collective-permute-start.33 = (f32[1,1,3,2]{2,3,1,0:T(2,128)S(1)}, f32[1,1,3,2]{2,3,1,0:T(2,128)S(1)}, u32[]{:S(2)}, u32[]{:S(2)}) collective-permute-start(f32[1,1,3,2]{2,3,1,0:T(2,128)S(1)} %bitcast.177), channel_id=1, source_target_pairs={{8,0},{16,8},{24,16},{32,24},{40,32},{48,40},{56,48},{64,56},{72,6... | collective-permute-start | bytes 80 | tf_op jit(solution)/shard_map/ppermute | solution.py:25
  301.5 4.3 %collective-permute-done.32 = f32[1,1,3,2]{2,3,1,0:T(2,128)S(1)} collective-permute-done((f32[1,1,3,2]{2,3,1,0:T(2,128)S(1)}, f32[1,1,3,2]{2,3,1,0:T(2,128)S(1)}, u32[]{:S(2)}, u32[]{:S(2)}) %collective-permute-start.32) | collective-permute-done | bytes 56 | tf_op jit(solution)/shard_map/ppermute | solution.py:24
  305.8 8.1 %collective-permute-start.35 = (f32[3,1,3,2]{2,3,1,0:T(2,128)S(1)}, f32[3,1,3,2]{2,3,1,0:T(2,128)S(1)}, u32[]{:S(2)}, u32[]{:S(2)}) collective-permute-start(f32[3,1,3,2]{2,3,1,0:T(2,128)S(1)} %pad_maximum_fusion.56), channel_id=1, source_target_pairs={{1,0},{2,1},{3,2},{4,3},{5,4},{6,5},{7,6},{9,8},{10,9},{11,10},{12... | collective-permute-start | bytes 224 | tf_op jit(solution)/shard_map/ppermute | solution.py:25
  315.9 7.2 %collective-permute-done.34 = f32[3,1,3,2]{2,3,1,0:T(2,128)S(1)} collective-permute-done((f32[3,1,3,2]{2,3,1,0:T(2,128)S(1)}, f32[3,1,3,2]{2,3,1,0:T(2,128)S(1)}, u32[]{:S(2)}, u32[]{:S(2)}) %collective-permute-start.34) | collective-permute-done | bytes 104 | tf_op jit(solution)/shard_map/ppermute | solution.py:24
  (192 shorter events, 62.8 us)
Async XLA Ops:
  1.4 67.0 %collective-permute-start.5 = (f32[3,1,8,128]{3,2,1,0:T(8,128)S(1)}, f32[3,1,8,128]{3,2,1,0:T(8,128)S(1)}, u32[]{:S(2)}, u32[]{:S(2)}) collective-permute-start(f32[3,1,8,128]{3,2,1,0:T(8,128)S(1)} %get-tuple-element.95), channel_id=1, source_target_pairs={{8,0},{16,8},{24,16},{32,24},{40,32},{48,40},{56,48},{64,56},{72,6... | collective-permute-start | bytes 36872 | tf_op jit(solution)/shard_map/ppermute | solution.py:25
  5.3 63.0 %collective-permute-start.3 = (f32[3,1,8,128]{3,2,1,0:T(8,128)S(1)}, f32[3,1,8,128]{3,2,1,0:T(8,128)S(1)}, u32[]{:S(2)}, u32[]{:S(2)}) collective-permute-start(f32[3,1,8,128]{3,2,1,0:T(8,128)S(1)} %get-tuple-element.96), channel_id=1, source_target_pairs={{0,8},{8,16},{16,24},{24,32},{32,40},{40,48},{48,56},{56,64},{64,7... | collective-permute-start | bytes 36872 | tf_op jit(solution)/shard_map/ppermute | solution.py:24
  8.1 46.1 %collective-permute-start.4 = (f32[1,8,128]{2,1,0:T(8,128)S(1)}, f32[1,8,128]{2,1,0:T(8,128)S(1)}, u32[]{:S(2)}, u32[]{:S(2)}) collective-permute-start(f32[1,8,128]{2,1,0:T(8,128)S(1)} %get-tuple-element.117), channel_id=1, source_target_pairs={{8,0},{16,8},{24,16},{32,24},{40,32},{48,40},{56,48},{64,56},{72,6... | collective-permute-start | bytes 12296 | tf_op jit(solution)/shard_map/ppermute | solution.py:25
  13.9 40.4 %collective-permute-start.2 = (f32[1,8,128]{2,1,0:T(8,128)S(1)}, f32[1,8,128]{2,1,0:T(8,128)S(1)}, u32[]{:S(2)}, u32[]{:S(2)}) collective-permute-start(f32[1,8,128]{2,1,0:T(8,128)S(1)} %get-tuple-element.118), channel_id=1, source_target_pairs={{0,8},{8,16},{16,24},{24,32},{32,40},{40,48},{48,56},{56,64},{64,7... | collective-permute-start | bytes 12296 | tf_op jit(solution)/shard_map/ppermute | solution.py:24
  54.3 8.7 %collective-permute-start.8 = (f32[10,1,128]{2,1,0:T(1,128)S(1)}, f32[10,1,128]{2,1,0:T(1,128)S(1)}, u32[]{:S(2)}, u32[]{:S(2)}) collective-permute-start(f32[10,1,128]{2,1,0:T(1,128)S(1)} %get-tuple-element.106), channel_id=1, source_target_pairs={{1,0},{2,1},{3,2},{4,3},{5,4},{6,5},{7,6},{9,8},{10,9},{11,10},{12... | collective-permute-start | bytes 15368 | tf_op jit(solution)/shard_map/ppermute | solution.py:25
  58.9 9.1 %collective-permute-start.6 = (f32[10,1,128]{2,1,0:T(1,128)S(1)}, f32[10,1,128]{2,1,0:T(1,128)S(1)}, u32[]{:S(2)}, u32[]{:S(2)}) collective-permute-start(f32[10,1,128]{2,1,0:T(1,128)S(1)} %get-tuple-element.107), channel_id=1, source_target_pairs={{0,1},{1,2},{2,3},{3,4},{4,5},{5,6},{6,7},{8,9},{9,10},{10,11},{11... | collective-permute-start | bytes 15368 | tf_op jit(solution)/shard_map/ppermute | solution.py:24
  60.9 7.5 %collective-permute-start = (f32[3,9,128]{2,1,0:T(8,128)S(1)}, f32[3,9,128]{2,1,0:T(8,128)S(1)}, u32[]{:S(2)}, u32[]{:S(2)}) collective-permute-start(f32[3,9,128]{2,1,0:T(8,128)S(1)} %slice_bitcast_fusion), channel_id=1, source_target_pairs={{0,8},{8,16},{16,24},{24,32},{32,40},{40,48},{48,56},{56,64},{64,7... | collective-permute-start | bytes 41480 | tf_op jit(solution)/shard_map/ppermute | solution.py:33
  68.4 12.3 %collective-permute-start.1 = (f32[3,8,128]{2,1,0:T(8,128)S(1)}, f32[3,8,128]{2,1,0:T(8,128)S(1)}, u32[]{:S(2)}, u32[]{:S(2)}) collective-permute-start(f32[3,8,128]{2,1,0:T(8,128)S(1)} %bitcast.171), channel_id=1, source_target_pairs={{0,1},{1,2},{2,3},{3,4},{4,5},{5,6},{6,7},{8,9},{9,10},{10,11},{11... | collective-permute-start | bytes 36872 | tf_op jit(solution)/shard_map/ppermute | solution.py:33
  71.2 9.6 %collective-permute-start.7 = (f32[3,10,1,128]{3,2,1,0:T(1,128)S(1)}, f32[3,10,1,128]{3,2,1,0:T(1,128)S(1)}, u32[]{:S(2)}, u32[]{:S(2)}) collective-permute-start(f32[3,10,1,128]{3,2,1,0:T(1,128)S(1)} %get-tuple-element.83), channel_id=1, source_target_pairs={{0,1},{1,2},{2,3},{3,4},{4,5},{5,6},{6,7},{8,9},{9,10},{10,11},{11... | collective-permute-start | bytes 46088 | tf_op jit(solution)/shard_map/ppermute | solution.py:24
  74.7 7.4 %collective-permute-start.9 = (f32[3,10,1,128]{3,2,1,0:T(1,128)S(1)}, f32[3,10,1,128]{3,2,1,0:T(1,128)S(1)}, u32[]{:S(2)}, u32[]{:S(2)}) collective-permute-start(f32[3,10,1,128]{3,2,1,0:T(1,128)S(1)} %get-tuple-element.84), channel_id=1, source_target_pairs={{1,0},{2,1},{3,2},{4,3},{5,4},{6,5},{7,6},{9,8},{10,9},{11,10},{12... | collective-permute-start | bytes 46088 | tf_op jit(solution)/shard_map/ppermute | solution.py:25
  82.6 7.7 %collective-permute-start.10 = (f32[3,1,8,128]{3,2,1,0:T(8,128)S(1)}, f32[3,1,8,128]{3,2,1,0:T(8,128)S(1)}, u32[]{:S(2)}, u32[]{:S(2)}) collective-permute-start(f32[3,1,8,128]{3,2,1,0:T(8,128)S(1)} %get-tuple-element.93), channel_id=1, source_target_pairs={{0,8},{8,16},{16,24},{24,32},{32,40},{40,48},{48,56},{56,64},{64,7... | collective-permute-start | bytes 36872 | tf_op jit(solution)/shard_map/ppermute | solution.py:24
  84.5 7.1 %collective-permute-start.11 = (f32[3,1,8,128]{3,2,1,0:T(8,128)S(1)}, f32[3,1,8,128]{3,2,1,0:T(8,128)S(1)}, u32[]{:S(2)}, u32[]{:S(2)}) collective-permute-start(f32[3,1,8,128]{3,2,1,0:T(8,128)S(1)} %get-tuple-element.94), channel_id=1, source_target_pairs={{8,0},{16,8},{24,16},{32,24},{40,32},{48,40},{56,48},{64,56},{72,6... | collective-permute-start | bytes 36872 | tf_op jit(solution)/shard_map/ppermute | solution.py:25
  91.7 9.8 %collective-permute-start.12 = (f32[3,10,1,128]{3,2,1,0:T(1,128)S(1)}, f32[3,10,1,128]{3,2,1,0:T(1,128)S(1)}, u32[]{:S(2)}, u32[]{:S(2)}) collective-permute-start(f32[3,10,1,128]{3,2,1,0:T(1,128)S(1)} %get-tuple-element.81), channel_id=1, source_target_pairs={{0,1},{1,2},{2,3},{3,4},{4,5},{5,6},{6,7},{8,9},{9,10},{10,11},{11... | collective-permute-start | bytes 46088 | tf_op jit(solution)/shard_map/ppermute | solution.py:24
  93.6 9.2 %collective-permute-start.13 = (f32[3,10,1,128]{3,2,1,0:T(1,128)S(1)}, f32[3,10,1,128]{3,2,1,0:T(1,128)S(1)}, u32[]{:S(2)}, u32[]{:S(2)}) collective-permute-start(f32[3,10,1,128]{3,2,1,0:T(1,128)S(1)} %get-tuple-element.82), channel_id=1, source_target_pairs={{1,0},{2,1},{3,2},{4,3},{5,4},{6,5},{7,6},{9,8},{10,9},{11,10},{12... | collective-permute-start | bytes 46088 | tf_op jit(solution)/shard_map/ppermute | solution.py:25
  103.3 7.7 %collective-permute-start.14 = (f32[3,1,8,128]{3,2,1,0:T(8,128)S(1)}, f32[3,1,8,128]{3,2,1,0:T(8,128)S(1)}, u32[]{:S(2)}, u32[]{:S(2)}) collective-permute-start(f32[3,1,8,128]{3,2,1,0:T(8,128)S(1)} %get-tuple-element.91), channel_id=1, source_target_pairs={{0,8},{8,16},{16,24},{24,32},{32,40},{40,48},{48,56},{56,64},{64,7... | collective-permute-start | bytes 36872 | tf_op jit(solution)/shard_map/ppermute | solution.py:24
  112.4 9.8 %collective-permute-start.16 = (f32[3,10,1,128]{3,2,1,0:T(1,128)S(1)}, f32[3,10,1,128]{3,2,1,0:T(1,128)S(1)}, u32[]{:S(2)}, u32[]{:S(2)}) collective-permute-start(f32[3,10,1,128]{3,2,1,0:T(1,128)S(1)} %get-tuple-element.79), channel_id=1, source_target_pairs={{0,1},{1,2},{2,3},{3,4},{4,5},{5,6},{6,7},{8,9},{9,10},{10,11},{11... | collective-permute-start | bytes 46088 | tf_op jit(solution)/shard_map/ppermute | solution.py:24
  114.4 9.2 %collective-permute-start.17 = (f32[3,10,1,128]{3,2,1,0:T(1,128)S(1)}, f32[3,10,1,128]{3,2,1,0:T(1,128)S(1)}, u32[]{:S(2)}, u32[]{:S(2)}) collective-permute-start(f32[3,10,1,128]{3,2,1,0:T(1,128)S(1)} %get-tuple-element.80), channel_id=1, source_target_pairs={{1,0},{2,1},{3,2},{4,3},{5,4},{6,5},{7,6},{9,8},{10,9},{11,10},{12... | collective-permute-start | bytes 46088 | tf_op jit(solution)/shard_map/ppermute | solution.py:25
  195.8 7.2 %collective-permute-start.18 = (f32[3,9,128]{2,0,1:T(4,128)S(1)}, f32[3,9,128]{2,0,1:T(4,128)S(1)}, u32[]{:S(2)}, u32[]{:S(2)}) collective-permute-start(f32[3,9,128]{2,0,1:T(4,128)S(1)} %get-tuple-element.73), channel_id=1, source_target_pairs={{0,8},{8,16},{16,24},{24,32},{32,40},{40,48},{48,56},{56,64},{64,7... | collective-permute-start | bytes 41480 | tf_op jit(solution)/shard_map/ppermute | solution.py:33
  203.1 9.5 %collective-permute-start.19 = (f32[3,8,128]{2,1,0:T(8,128)S(1)}, f32[3,8,128]{2,1,0:T(8,128)S(1)}, u32[]{:S(2)}, u32[]{:S(2)}) collective-permute-start(f32[3,8,128]{2,1,0:T(8,128)S(1)} %get-tuple-element.85), channel_id=1, source_target_pairs={{0,1},{1,2},{2,3},{3,4},{4,5},{5,6},{6,7},{8,9},{9,10},{10,11},{11... | collective-permute-start | bytes 36872 | tf_op jit(solution)/shard_map/ppermute | solution.py:33
  205.2 15.3 %collective-permute-start.29 = (f32[1,1,3,2]{2,3,1,0:T(2,128)S(1)}, f32[1,1,3,2]{2,3,1,0:T(2,128)S(1)}, u32[]{:S(2)}, u32[]{:S(2)}) collective-permute-start(f32[1,1,3,2]{2,3,1,0:T(2,128)S(1)} %bitcast.173), channel_id=1, source_target_pairs={{8,0},{16,8},{24,16},{32,24},{40,32},{48,40},{56,48},{64,56},{72,6... | collective-permute-start | bytes 80 | tf_op jit(solution)/shard_map/ppermute | solution.py:25
  207.1 13.4 %collective-permute-start.28 = (f32[1,1,3,2]{2,3,1,0:T(2,128)S(1)}, f32[1,1,3,2]{2,3,1,0:T(2,128)S(1)}, u32[]{:S(2)}, u32[]{:S(2)}) collective-permute-start(f32[1,1,3,2]{2,3,1,0:T(2,128)S(1)} %bitcast.174), channel_id=1, source_target_pairs={{0,8},{8,16},{16,24},{24,32},{32,40},{40,48},{48,56},{56,64},{64,7... | collective-permute-start | bytes 80 | tf_op jit(solution)/shard_map/ppermute | solution.py:24
  212.8 14.5 %collective-permute-start.20 = (f32[3,1,8,128]{3,2,1,0:T(8,128)S(1)}, f32[3,1,8,128]{3,2,1,0:T(8,128)S(1)}, u32[]{:S(2)}, u32[]{:S(2)}) collective-permute-start(f32[3,1,8,128]{3,2,1,0:T(8,128)S(1)} %get-tuple-element.89), channel_id=1, source_target_pairs={{0,8},{8,16},{16,24},{24,32},{32,40},{40,48},{48,56},{56,64},{64,7... | collective-permute-start | bytes 36872 | tf_op jit(solution)/shard_map/ppermute | solution.py:24
  214.7 12.6 %collective-permute-start.21 = (f32[3,1,8,128]{3,2,1,0:T(8,128)S(1)}, f32[3,1,8,128]{3,2,1,0:T(8,128)S(1)}, u32[]{:S(2)}, u32[]{:S(2)}) collective-permute-start(f32[3,1,8,128]{3,2,1,0:T(8,128)S(1)} %get-tuple-element.90), channel_id=1, source_target_pairs={{8,0},{16,8},{24,16},{32,24},{40,32},{48,40},{56,48},{64,56},{72,6... | collective-permute-start | bytes 36872 | tf_op jit(solution)/shard_map/ppermute | solution.py:25
  220.5 16.3 %collective-permute-start.31 = (f32[3,1,3,2]{2,3,1,0:T(2,128)S(1)}, f32[3,1,3,2]{2,3,1,0:T(2,128)S(1)}, u32[]{:S(2)}, u32[]{:S(2)}) collective-permute-start(f32[3,1,3,2]{2,3,1,0:T(2,128)S(1)} %pad_maximum_fusion.55), channel_id=1, source_target_pairs={{1,0},{2,1},{3,2},{4,3},{5,4},{6,5},{7,6},{9,8},{10,9},{11,10},{12... | collective-permute-start | bytes 224 | tf_op jit(solution)/shard_map/ppermute | solution.py:25
  225.4 11.5 %collective-permute-start.30 = (f32[3,1,3,2]{2,3,1,0:T(2,128)S(1)}, f32[3,1,3,2]{2,3,1,0:T(2,128)S(1)}, u32[]{:S(2)}, u32[]{:S(2)}) collective-permute-start(f32[3,1,3,2]{2,3,1,0:T(2,128)S(1)} %pad_maximum_fusion.55), channel_id=1, source_target_pairs={{0,1},{1,2},{2,3},{3,4},{4,5},{5,6},{6,7},{8,9},{9,10},{10,11},{11... | collective-permute-start | bytes 224 | tf_op jit(solution)/shard_map/ppermute | solution.py:24
  227.4 9.5 %collective-permute-start.22 = (f32[3,10,1,128]{3,2,1,0:T(1,128)S(1)}, f32[3,10,1,128]{3,2,1,0:T(1,128)S(1)}, u32[]{:S(2)}, u32[]{:S(2)}) collective-permute-start(f32[3,10,1,128]{3,2,1,0:T(1,128)S(1)} %get-tuple-element.77), channel_id=1, source_target_pairs={{0,1},{1,2},{2,3},{3,4},{4,5},{5,6},{6,7},{8,9},{9,10},{10,11},{11... | collective-permute-start | bytes 46088 | tf_op jit(solution)/shard_map/ppermute | solution.py:24
  229.3 9.0 %collective-permute-start.23 = (f32[3,10,1,128]{3,2,1,0:T(1,128)S(1)}, f32[3,10,1,128]{3,2,1,0:T(1,128)S(1)}, u32[]{:S(2)}, u32[]{:S(2)}) collective-permute-start(f32[3,10,1,128]{3,2,1,0:T(1,128)S(1)} %get-tuple-element.78), channel_id=1, source_target_pairs={{1,0},{2,1},{3,2},{4,3},{5,4},{6,5},{7,6},{9,8},{10,9},{11,10},{12... | collective-permute-start | bytes 46088 | tf_op jit(solution)/shard_map/ppermute | solution.py:25
  238.8 7.9 %collective-permute-start.24 = (f32[3,1,8,128]{3,2,1,0:T(8,128)S(1)}, f32[3,1,8,128]{3,2,1,0:T(8,128)S(1)}, u32[]{:S(2)}, u32[]{:S(2)}) collective-permute-start(f32[3,1,8,128]{3,2,1,0:T(8,128)S(1)} %get-tuple-element.87), channel_id=1, source_target_pairs={{0,8},{8,16},{16,24},{24,32},{32,40},{40,48},{48,56},{56,64},{64,7... | collective-permute-start | bytes 36872 | tf_op jit(solution)/shard_map/ppermute | solution.py:24
  247.9 10.0 %collective-permute-start.26 = (f32[3,10,1,128]{3,2,1,0:T(1,128)S(1)}, f32[3,10,1,128]{3,2,1,0:T(1,128)S(1)}, u32[]{:S(2)}, u32[]{:S(2)}) collective-permute-start(f32[3,10,1,128]{3,2,1,0:T(1,128)S(1)} %get-tuple-element.75), channel_id=1, source_target_pairs={{0,1},{1,2},{2,3},{3,4},{4,5},{5,6},{6,7},{8,9},{9,10},{10,11},{11... | collective-permute-start | bytes 46088 | tf_op jit(solution)/shard_map/ppermute | solution.py:24
  249.8 9.2 %collective-permute-start.27 = (f32[3,10,1,128]{3,2,1,0:T(1,128)S(1)}, f32[3,10,1,128]{3,2,1,0:T(1,128)S(1)}, u32[]{:S(2)}, u32[]{:S(2)}) collective-permute-start(f32[3,10,1,128]{3,2,1,0:T(1,128)S(1)} %get-tuple-element.76), channel_id=1, source_target_pairs={{1,0},{2,1},{3,2},{4,3},{5,4},{6,5},{7,6},{9,8},{10,9},{11,10},{12... | collective-permute-start | bytes 46088 | tf_op jit(solution)/shard_map/ppermute | solution.py:25
  305.8 10.0 %collective-permute-start.35 = (f32[3,1,3,2]{2,3,1,0:T(2,128)S(1)}, f32[3,1,3,2]{2,3,1,0:T(2,128)S(1)}, u32[]{:S(2)}, u32[]{:S(2)}) collective-permute-start(f32[3,1,3,2]{2,3,1,0:T(2,128)S(1)} %pad_maximum_fusion.56), channel_id=1, source_target_pairs={{1,0},{2,1},{3,2},{4,3},{5,4},{6,5},{7,6},{9,8},{10,9},{11,10},{12... | collective-permute-start | bytes 224 | tf_op jit(solution)/shard_map/ppermute | solution.py:25
  313.9 9.1 %collective-permute-start.34 = (f32[3,1,3,2]{2,3,1,0:T(2,128)S(1)}, f32[3,1,3,2]{2,3,1,0:T(2,128)S(1)}, u32[]{:S(2)}, u32[]{:S(2)}) collective-permute-start(f32[3,1,3,2]{2,3,1,0:T(2,128)S(1)} %pad_maximum_fusion.56), channel_id=1, source_target_pairs={{0,1},{1,2},{2,3},{3,4},{4,5},{5,6},{6,7},{8,9},{9,10},{10,11},{11... | collective-permute-start | bytes 224 | tf_op jit(solution)/shard_map/ppermute | solution.py:24
  (14 other events, 161.5 us)
where the time goes:
time: 325 us; the launch traced here: 324 us
  matrix products  143 us (44%)
  starting transfers between devices  135 us (42%)
  waiting for transfers between devices  35.2 us (11%)
  other arithmetic  5.56 us (2%)
    ppermute x16, starting transfers between devices, extended(): after = lax.ppermute(first, axis, down)  93.7 us
    dot_general x6, matrix products, local(): jnp.dot(write_plane.T, scaled, precision=lax.Precision.HIGHEST)  72.9 us
    dot_general x6, matrix products, local(): jnp.dot(read_plane, plane_vel[comp], precision=lax.Precision.HIGHEST)  69.2 us
    ppermute x16, starting transfers between devices, extended(): before = lax.ppermute(last, axis, up)  32.8 us
    ppermute x16, waiting for transfers between devices, extended(): before = lax.ppermute(last, axis, up)  16.6 us
    ppermute x16, waiting for transfers between devices, extended(): after = lax.ppermute(first, axis, down)  10.5 us
    ppermute x4, starting transfers between devices, passed_along(): return lax.ppermute(array, axis, pairs)  8.68 us
    ppermute x4, waiting for transfers between devices, passed_along(): return lax.ppermute(array, axis, pairs)  8.08 us
  transfers between devices with their start and end apart: 36, of which 13 were waited for; matrix products, arithmetic and copies ran while one was open for 13% of the time, Pallas kernels for 0%

commit v1 on v0

v1 whole, which is shorter than its diff:
```python
import jax
import jax.numpy as jnp
from jax import lax
from jax.experimental import pallas as pl
from jax.experimental.pallas import tpu as pltpu
from jax.sharding import PartitionSpec as P

ITERS = 2
MESH = pl.DeviceIdType.MESH
F32 = jnp.float32
BF16 = jnp.bfloat16

CX, CY, NZ = 8, 8, 128
SPH, MARK = 2, 2048
CHUNK = 512
PER_SPHERE = MARK // CHUNK
CHUNKS = SPH * PER_SPHERE
ROWS = 88
PAD = 272
EXT = 13 * 16
HALO0, FORCE0, HALO1, FORCE1, RIGID0, RIGID1 = range(6)
OTHERS = [0, 1, 2, 3, 5, 6, 7, 8]


def row(x, y):
    return (x + 2) * 16 + y % 16


def split(value):
    high = value.astype(BF16)
    low = (value - high.astype(F32)).astype(BF16)
    return high, low


def body(
    vel, force, visc_class, table, mult, cell, frac, pair_sphere, pair_partner, normal, gap, contact,
    vel_out, mult_out, contact_out,
    own, ext, pack, halo_in, coef, rhs, grid, grid_pack, grid_diag, grid_in, diag_in,
    acc, share_acc, share, plane_w, depth_w, stack, left, mult_mid, rigid, rigid_in, normal8, contact_mid,
    send_sem, recv_sem,
):
    wide, narrow = lax.axis_index("wide"), lax.axis_index("narrow")
    n_wide, n_narrow = lax.axis_size("wide"), lax.axis_size("narrow")

    def neighbour(d):
        dx, dy = d // 3 - 1, d % 3 - 1
        return (lax.rem(wide + dx + n_wide, n_wide), lax.rem(narrow + dy + n_narrow, n_narrow))

    barrier = pltpu.get_barrier_semaphore()
    for d in OTHERS:
        pl.semaphore_signal(barrier, inc=1, device_id=neighbour(d), device_id_type=MESH)

    def transfer(kind, s, src, dst):
        return pltpu.make_async_remote_copy(
            src_ref=src, dst_ref=dst, send_sem=send_sem.at[kind, s], recv_sem=recv_sem.at[kind, s],
            device_id=neighbour(8 - s), device_id_type=MESH,
        )

    def halo_copies(turn):
        fields = 4 if turn == 0 else 3
        copies = []
        for s in OTHERS:
            dx, dy = s // 3 - 1, s % 3 - 1
            if dy == 0:
                rows = 24 if dx == 1 else 16
                start = 0 if dx == 1 else 48
                src = own.at[turn, 0:fields, start:start + rows]
            else:
                rows = 24 if dy == 1 else 16
                src = pack.at[turn, 0 if dy == 1 else 1, 0:fields, 0:rows]
            copies.append(transfer(HALO0 if turn == 0 else HALO1, s, src, halo_in.at[turn, s, 0:fields, 0:rows]))
        return copies

    def force_copies(turn):
        copies = []
        for s in OTHERS:
            dx, dy = s // 3 - 1, s % 3 - 1
            if dx != 0 and dy != 0:
                src, dst = grid_diag.at[turn, s], diag_in.at[turn, s]
            elif dy == 0:
                start = 0 if dx == 1 else 64
                src, dst = grid.at[turn, :, start:start + 24], grid_in.at[turn, s]
            else:
                src, dst = grid_pack.at[turn, 0 if dy == 1 else 1], grid_in.at[turn, s]
            copies.append(transfer(FORCE0 if turn == 0 else FORCE1, s, src, dst))
        return copies

    def rigid_copies(turn):
        return [
            transfer(RIGID0 if turn == 0 else RIGID1, s, rigid.at[turn], rigid_in.at[turn, s]) for s in OTHERS
        ]

    def start(copies):
        for copy in copies:
            copy.start()

    def arrive(copies):
        for copy in copies:
            copy.wait_recv()

    def leave(copies):
        for copy in copies:
            copy.wait_send()

    def pack_halo(turn):
        fields = 4 if turn == 0 else 3
        for f in range(fields):
            for j in range(3):
                pack[turn, 0, f, 8 * j:8 * j + 8, :] = own[turn, f, pl.ds(j, 8, stride=8), :]
            for j in range(2):
                pack[turn, 1, f, 8 * j:8 * j + 8, :] = own[turn, f, pl.ds(6 + j, 8, stride=8), :]

    def unpack_halo(turn):
        fields = 4 if turn == 0 else 3
        for f in range(fields):
            for i in range(3):
                ext[turn, f, pl.ds(row(8 + i, 0), 8), :] = halo_in[turn, 7, f, 8 * i:8 * i + 8, :]
            for i in range(2):
                ext[turn, f, pl.ds(row(i - 2, 0), 8), :] = halo_in[turn, 1, f, 8 * i:8 * i + 8, :]
            for j in range(3):
                ext[turn, f, pl.ds(row(0, 8 + j), 8, stride=16), :] = halo_in[turn, 5, f, 8 * j:8 * j + 8, :]
                ext[turn, f, pl.ds(row(8, 8 + j), 3, stride=16), :] = halo_in[turn, 8, f, 8 * j:8 * j + 3, :]
                ext[turn, f, pl.ds(row(-2, 8 + j), 2, stride=16), :] = halo_in[turn, 2, f, 8 * j + 6:8 * j + 8, :]
            for j in range(2):
                ext[turn, f, pl.ds(row(0, j - 2), 8, stride=16), :] = halo_in[turn, 3, f, 8 * j:8 * j + 8, :]
                ext[turn, f, pl.ds(row(8, j - 2), 3, stride=16), :] = halo_in[turn, 6, f, 8 * j:8 * j + 3, :]
                ext[turn, f, pl.ds(row(-2, j - 2), 2, stride=16), :] = halo_in[turn, 0, f, 8 * j + 6:8 * j + 8, :]

    classes = visc_class[...]
    mu = jnp.where(classes == 0, table[0], jnp.where(classes == 1, table[1], jnp.where(classes == 2, table[2], table[3])))
    mu = jnp.where((classes >= 0) & (classes <= 3), mu, F32(0.0))
    own[0, 3, :, :] = mu
    for c in range(3):
        own[0, c, :, :] = vel[c]
    for f in range(4):
        for x in range(8):
            ext[0, f, pl.ds(row(x, 0), 8), :] = own[0, f, 8 * x:8 * x + 8, :]
    pack_halo(0)

    pl.semaphore_wait(barrier, 8)
    start(halo_copies(0))

    acc[...] = jnp.zeros_like(acc)
    share_acc[...] = jnp.zeros_like(share_acc)

    def add_spread(lhs, depth):
        high, low = split(lhs)
        dims = (((1,), (1,)), ((), ()))
        return lax.dot_general(high, depth, dims, preferred_element_type=F32) + lax.dot_general(
            low, depth, dims, preferred_element_type=F32
        )

    def setup(n, carry):
        s, k = n // PER_SPHERE, n % PER_SPHERE
        lanes = pl.ds(pl.multiple_of(k * CHUNK, CHUNK), CHUNK)
        spot = cell[pl.ds(s, 1), lanes]
        cell_x, cell_y, cell_z = spot >> 10, (spot >> 7) & 7, spot & 127
        frac_x, frac_y, frac_z = (frac[a, pl.ds(s, 1), lanes] for a in range(3))
        gap_z = lax.broadcasted_iota(jnp.int32, (NZ, CHUNK), 0) - cell_z
        depth = jnp.where(gap_z == 0, 1.0 - frac_z, jnp.where(gap_z == 1, frac_z, F32(0.0)))
        depth_high, depth_low = split(depth)
        depth_w[n, 0:NZ, :] = depth_high
        depth_w[n, NZ:2 * NZ, :] = depth_low
        next_x = jnp.where(wide == n_wide - 1, F32(0.0), frac_x)
        next_y = jnp.where(narrow == n_narrow - 1, F32(0.0), frac_y)
        gap_8 = lax.broadcasted_iota(jnp.int32, (8, CHUNK), 0)
        weight_y = jnp.where(gap_8 == cell_y, 1.0 - frac_y, jnp.where(gap_8 == cell_y + 1, frac_y, F32(0.0)))
        weight_x = jnp.where(gap_8 == cell_x, 1.0 - frac_x, jnp.where(gap_8 == cell_x + 1, frac_x, F32(0.0)))
        last_x = jnp.where(cell_x == 7, next_x, F32(0.0))
        last_y = jnp.where(cell_y == 7, next_y, F32(0.0))
        tiles = [weight_x * last_y]
        for x in range(8):
            tiles.append(weight_x[x:x + 1] * weight_y)
        tiles.append(last_x * weight_y)
        corner = jnp.where(gap_8 == 0, weight_x[7:8], jnp.where(gap_8 == 1, last_x, F32(0.0))) * last_y
        tiles.append(corner)
        weight = jnp.concatenate(tiles, axis=0)
        plane_w[n] = weight
        lhs = [weight * (0.25 * mult[c, pl.ds(s, 1), lanes]) for c in range(3)]
        result = add_spread(jnp.concatenate(lhs + [weight], axis=0), depth_w[n])
        acc[0:264, :] += result[0:264]
        share_acc[s] += result[264:352]
        return carry

    lax.fori_loop(0, CHUNKS, setup, 0)
    for s in range(SPH):
        share[s] = (share_acc[s, :, 0:NZ] + share_acc[s, :, NZ:2 * NZ]) * F32(1.0 / MARK)

    def send_force(turn):
        for c in range(3):
            base = c * ROWS
            for t in range(11):
                part = acc[base + 8 * t:base + 8 * t + 8, 0:NZ] + acc[base + 8 * t:base + 8 * t + 8, NZ:2 * NZ]
                if 1 <= t <= 8:
                    part = part + force[c, 8 * t - 8:8 * t, :]
                grid[turn, c, 8 * t:8 * t + 8, :] = part
            for j in range(2):
                grid_pack[turn, 0, c, 8 * j:8 * j + 8, :] = grid[turn, c, pl.ds(8 + j, 8, stride=8), :]
            grid_pack[turn, 0, c, 16:24, :] = grid[turn, c, 72:80, :]
            grid_pack[turn, 1, c, 0:8, :] = grid[turn, c, pl.ds(15, 8, stride=8), :]
            grid_pack[turn, 1, c, 8:16, :] = grid[turn, c, 0:8, :]
            grid_pack[turn, 1, c, 16:17, :] = grid[turn, c, 79:80, :]
            grid_pack[turn, 1, c, 17:18, :] = grid[turn, c, 81:82, :]
            for s in (0, 2, 6, 8):
                dx, dy = s // 3 - 1, s % 3 - 1
                first = 8 if dx == 1 else 64
                for j in range(2):
                    if dy == 1:
                        rows = grid[turn, c, pl.ds(first + j, 2, stride=8), :]
                    elif j == 0:
                        rows = grid[turn, c, pl.ds(first + 7, 2, stride=8), :]
                    else:
                        at = 0 if dx == 1 else 80
                        rows = grid[turn, c, at:at + 2, :]
                    grid_diag[turn, s, 4 * c + 2 * j:4 * c + 2 * j + 2, :] = rows
        start(force_copies(turn))

    send_force(0)

    halos = halo_copies(0)
    arrive(halos)
    unpack_halo(0)
    row_id = lax.broadcasted_iota(jnp.int32, (16, NZ), 0)
    lane_id = lax.broadcasted_iota(jnp.int32, (16, NZ), 1)
    y_id = narrow * CY + jnp.where(row_id > 11, row_id - 16, row_id)

    def in_y(y):
        return (y >= 0) & (y < n_narrow * CY)

    def coefficients(i, carry):
        def viscosity(shift):
            x = wide * CX + i - 1 + shift
            inside = in_y(y_id) & (x >= 0) & (x < n_wide * CX)
            at = pl.multiple_of((i + 1 + shift) * 16, 16)
            return jnp.where(inside, ext[0, 3, pl.ds(at, 16), :], F32(0.0))

        mid = viscosity(0)
        x = wide * CX + i - 1
        around = [
            viscosity(-1),
            viscosity(1),
            jnp.where(in_y(y_id - 1), pltpu.roll(mid, 1, 0), F32(0.0)),
            jnp.where(in_y(y_id + 1), pltpu.roll(mid, 15, 0), F32(0.0)),
            jnp.where(lane_id == 0, F32(0.0), pltpu.roll(mid, 1, 1)),
            jnp.where(lane_id == NZ - 1, F32(0.0), pltpu.roll(mid, NZ - 1, 1)),
        ]
        valid = [
            (x - 1 >= 0) & (lane_id >= 0),
            (x + 1 < n_wide * CX) & (lane_id >= 0),
            in_y(y_id - 1),
            in_y(y_id + 1),
            lane_id > 0,
            lane_id < NZ - 1,
        ]
        faces = [0.5 * (mid + other) for other in around]
        diagonal = 1.0 + faces[0] + faces[1] + faces[2] + faces[3] + faces[4] + faces[5]
        inside = in_y(y_id) & (x >= 0) & (x < n_wide * CX)
        inverse = jnp.where(inside, 1.0 / diagonal, F32(0.0))
        at = pl.ds(pl.multiple_of(i * 16, 16), 16)
        for a in range(6):
            coef[a, at, :] = jnp.where(valid[a], faces[a] * inverse, F32(0.0))
        coef[6, at, :] = inverse
        return carry

    lax.fori_loop(0, 11, coefficients, 0)
    rhs[...] = jnp.zeros_like(rhs)
    stack[...] = jnp.zeros_like(stack)
    normal8[...] = jnp.zeros_like(normal8)
    normal8[0:3, :] = normal[...]
    normal8[4:7, :] = normal[...]

    sphere_row = lax.broadcasted_iota(jnp.int32, (8, 32), 0) // 4
    pair_s = pair_sphere[...].reshape(1, 32)
    pair_q = pair_partner[...].reshape(1, 32)
    contact_mid[...] = contact[...].reshape(1, 32)
    pair_gap = gap[...].reshape(1, 32)

    def gather_force(turn):
        arrive(force_copies(turn))
        for c in range(3):
            def add(x, y, n, stride, value):
                at = pl.ds(row(x, y), n, stride=stride) if stride != 1 else pl.ds(row(x, y), n)
                rhs[turn, c, at, :] += value

            for x in range(9):
                rhs[turn, c, pl.ds(row(x, 0), 8), :] = grid[turn, c, 8 + 8 * x:16 + 8 * x, :]
            rhs[turn, c, pl.ds(row(0, 8), 8, stride=16), :] = grid[turn, c, 0:8, :]
            rhs[turn, c, pl.ds(row(8, 8), 1), :] = grid[turn, c, 81:82, :]
            add(8, 0, 8, 1, grid_in[turn, 7, c, 8:16, :])
            add(9, 0, 8, 1, grid_in[turn, 7, c, 16:24, :])
            add(8, 8, 2, 16, grid_in[turn, 7, c, 0:2, :])
            add(-1, 0, 8, 1, grid_in[turn, 1, c, 0:8, :])
            add(0, 0, 8, 1, grid_in[turn, 1, c, 8:16, :])
            add(-1, 8, 2, 16, grid_in[turn, 1, c, 16:18, :])
            for s, low in ((5, 8), (3, -1)):
                for j in range(2):
                    add(0, low + j, 8, 16, grid_in[turn, s, c, 8 * j:8 * j + 8, :])
                    add(8, low + j, 1, 1, grid_in[turn, s, c, 16 + j:17 + j, :])
            for s in (0, 2, 6, 8):
                x = 8 if s // 3 == 2 else -1
                y = 8 if s % 3 == 2 else -1
                for j in range(2):
                    add(x, y + j, 2, 16, diag_in[turn, s, 4 * c + 2 * j:4 * c + 2 * j + 2, :])

    def sweep(source, target, first, count, turn):
        def one(i, carry):
            at = pl.ds(pl.multiple_of(i * 16, 16), 16)
            factors = [coef[a, at, :] for a in range(7)]
            for c in range(3):
                def load(shift):
                    return source[c, pl.ds(pl.multiple_of((i + 1 + shift) * 16, 16), 16), :]

                mid = load(0)
                value = factors[6] * rhs[turn, c, pl.ds(pl.multiple_of((i + 1) * 16, 16), 16), :]
                value += factors[0] * load(-1)
                value += factors[1] * load(1)
                value += factors[2] * pltpu.roll(mid, 1, 0)
                value += factors[3] * pltpu.roll(mid, 15, 0)
                value += factors[4] * pltpu.roll(mid, 1, 1)
                value += factors[5] * pltpu.roll(mid, NZ - 1, 1)
                target[c, pl.ds(pl.multiple_of((i + 1) * 16, 16), 16), :] = value
            return carry

        lax.fori_loop(first, first + count, one, 0)

    def update_contact(turn):
        quarter = pair_q // 2
        partner = jnp.zeros((8, 32), F32)
        for q in range(9):
            if q == 4:
                tile = rigid[turn, :, 0:32]
            else:
                qx, qy = q // 3 - 1, q % 3 - 1
                inside = (wide + qx >= 0) & (wide + qx < n_wide) & (narrow + qy >= 0) & (narrow + qy < n_narrow)
                tile = jnp.where(inside, rigid_in[turn, q, :, 0:32], F32(0.0))
            partner = jnp.where(quarter == q, tile, partner)
        closing8 = jnp.where(sphere_row == pair_q - 2 * quarter, partner, F32(0.0)) - jnp.where(
            sphere_row == pair_s, rigid[turn, :, 0:32], F32(0.0)
        )
        closing = jnp.sum(normal8[...] * closing8, axis=0, keepdims=True)
        return jnp.maximum(F32(0.0), contact_mid[...] - 0.5 * (pair_gap + closing))

    for turn in range(ITERS):
        last = turn == ITERS - 1
        if turn > 0:
            arrive(halo_copies(turn))
            unpack_halo(turn)
        gather_force(turn)
        middle = ext.at[2]
        sweep(ext.at[turn], middle, 0, 11, turn)
        sweep(middle, ext.at[3], 1, 9, turn)
        done = ext.at[3]
        for c in range(3):
            for x in range(9):
                tile = done[c, pl.ds(row(x, 0), 8), :]
                stack[c * ROWS + 8 + 8 * x:c * ROWS + 16 + 8 * x, :] = tile
                if x < 8:
                    if last:
                        vel_out[c, 8 * x:8 * x + 8, :] = tile
                    else:
                        own[turn + 1, c, 8 * x:8 * x + 8, :] = tile
                        ext[turn + 1, c, pl.ds(row(x, 0), 8), :] = tile
            stack[c * ROWS:c * ROWS + 8, :] = done[c, pl.ds(row(0, 8), 8, stride=16), :]
            stack[c * ROWS + 81:c * ROWS + 82, :] = done[c, pl.ds(row(8, 8), 1), :]
        if not last:
            pack_halo(turn + 1)
            start(halo_copies(turn + 1))
        if turn > 0:
            arrive(rigid_copies(turn - 1))
            contact_mid[...] = update_contact(turn - 1)
        sums = jnp.zeros((8, NZ), F32)
        row8 = lax.broadcasted_iota(jnp.int32, (8, NZ), 0)
        for s in range(SPH):
            for c in range(3):
                part = jnp.sum(share[s] * stack[c * ROWS:(c + 1) * ROWS, :], axis=0, keepdims=True)
                sums = jnp.where(row8 == 4 * s + c, part, sums)
        push = jnp.where(sphere_row == pair_s, normal8[...] * contact_mid[...], F32(0.0))
        speed = jnp.sum(sums, axis=1, keepdims=True) + 0.5 * jnp.sum(push, axis=1, keepdims=True)
        rigid[turn] = jnp.broadcast_to(speed, (8, NZ))
        start(rigid_copies(turn))
        high, low = split(stack[...])
        left[0:PAD, 0:NZ] = high
        left[0:PAD, NZ:2 * NZ] = high
        left[PAD:2 * PAD, 0:NZ] = low
        left[PAD:2 * PAD, NZ:2 * NZ] = low
        if not last:
            acc[...] = jnp.zeros_like(acc)
        source = mult if turn == 0 else mult_mid

        def markers(n, carry):
            s, k = n // PER_SPHERE, n % PER_SPHERE
            lanes = pl.ds(pl.multiple_of(k * CHUNK, CHUNK), CHUNK)
            weight = plane_w[n]
            sampled = jnp.dot(left[...], depth_w[n], preferred_element_type=F32)
            lhs = []
            for c in range(3):
                rows = slice(c * ROWS, (c + 1) * ROWS)
                low_rows = slice(PAD + c * ROWS, PAD + (c + 1) * ROWS)
                read = jnp.sum((sampled[rows] + sampled[low_rows]) * weight, axis=0, keepdims=True)
                speed = rigid[turn, pl.ds(4 * s + c, 1), 0:1]
                new = source[c, pl.ds(s, 1), lanes] + 0.5 * (speed - read)
                if last:
                    mult_out[c, pl.ds(s, 1), lanes] = new
                else:
                    mult_mid[c, pl.ds(s, 1), lanes] = new
                    lhs.append(weight * (0.25 * new))
            if not last:
                lhs.append(jnp.zeros((8, CHUNK), F32))
                acc[...] += add_spread(jnp.concatenate(lhs, axis=0), depth_w[n])
            return carry

        lax.fori_loop(0, CHUNKS, markers, 0)
        if not last:
            send_force(turn + 1)
    arrive(rigid_copies(ITERS - 1))
    contact_out[...] = update_contact(ITERS - 1).reshape(32)
    for turn in range(ITERS):
        leave(halo_copies(turn))
        leave(force_copies(turn))
        leave(rigid_copies(turn))


def local(
    velocity, force, visc_class, visc_table, multiplier, marker_cell, marker_frac,
    pair_sphere, pair_partner, pair_normal, pair_gap, contact_force,
):
    comps = 3
    vmem = pl.BlockSpec(memory_space=pltpu.VMEM)
    specs = [vmem] * 12
    specs[3] = pl.BlockSpec(memory_space=pltpu.SMEM)
    out = pl.pallas_call(
        body,
        out_shape=(
            jax.ShapeDtypeStruct((comps, CX * CY, NZ), F32),
            jax.ShapeDtypeStruct(multiplier.shape, F32),
            jax.ShapeDtypeStruct(contact_force.shape, F32),
        ),
        in_specs=specs,
        out_specs=(vmem, vmem, vmem),
        scratch_shapes=[
            pltpu.VMEM((2, 4, CX * CY, NZ), F32),
            pltpu.VMEM((4, 4, EXT, NZ), F32),
            pltpu.VMEM((2, 2, 4, 24, NZ), F32),
            pltpu.VMEM((2, 9, 4, 24, NZ), F32),
            pltpu.VMEM((7, 11 * 16, NZ), F32),
            pltpu.VMEM((2, comps, EXT, NZ), F32),
            pltpu.VMEM((2, comps, ROWS, NZ), F32),
            pltpu.VMEM((2, 2, comps, 24, NZ), F32),
            pltpu.VMEM((2, 9, 16, NZ), F32),
            pltpu.VMEM((2, 9, comps, 24, NZ), F32),
            pltpu.VMEM((2, 9, 16, NZ), F32),
            pltpu.VMEM((PAD, 2 * NZ), F32),
            pltpu.VMEM((SPH, ROWS, 2 * NZ), F32),
            pltpu.VMEM((SPH, ROWS, NZ), F32),
            pltpu.VMEM((CHUNKS, ROWS, CHUNK), F32),
            pltpu.VMEM((CHUNKS, 2 * NZ, CHUNK), BF16),
            pltpu.VMEM((PAD, NZ), F32),
            pltpu.VMEM((2 * PAD, 2 * NZ), BF16),
            pltpu.VMEM((comps, SPH, MARK), F32),
            pltpu.VMEM((2, 8, NZ), F32),
            pltpu.VMEM((2, 9, 8, NZ), F32),
            pltpu.VMEM((8, 32), F32),
            pltpu.VMEM((1, 32), F32),
            pltpu.SemaphoreType.DMA((6, 9)),
            pltpu.SemaphoreType.DMA((6, 9)),
        ],
        compiler_params=pltpu.CompilerParams(
            collective_id=0, has_side_effects=True, vmem_limit_bytes=48 * 1024 * 1024
        ),
    )(
        velocity.reshape(comps, CX * CY, NZ), force.reshape(comps, CX * CY, NZ), visc_class.reshape(CX * CY, NZ),
        visc_table, multiplier, marker_cell, marker_frac, pair_sphere, pair_partner, pair_normal, pair_gap, contact_force,
    )
    return (out[0].reshape(comps, CX, CY, NZ), out[1], out[2])


def solution(mesh):
    in_specs = (
        P(None, "wide", "narrow", None),
        P(None, "wide", "narrow", None),
        P("wide", "narrow", None),
        P(),
        P(None, ("wide", "narrow"), None),
        P(("wide", "narrow"), None),
        P(None, ("wide", "narrow"), None),
        P(("wide", "narrow")),
        P(("wide", "narrow")),
        P(None, ("wide", "narrow")),
        P(("wide", "narrow")),
        P(("wide", "narrow")),
    )
    out_specs = (
        P(None, "wide", "narrow", None),
        P(None, ("wide", "narrow"), None),
        P(("wide", "narrow")),
    )
    return jax.shard_map(local, mesh=mesh, in_specs=in_specs, out_specs=out_specs, check_vma=False)
```

time: 325 us -> 46.9 us (0.14)
  the two profiles are of different devices: /device:TPU:96 before, /device:TPU:1 now
where the time goes in v1:
time: 46.9 us; the launch traced here: 46.5 us
  Pallas kernels  38.5 us (82%)
  local copies, waits for them, and re-layouts  7.31 us (16%)
  between operations  0.7 us (1%)
    pallas_call x1, Pallas kernels, local(): pl.pallas_call(body, out_shape=(jax.ShapeDtypeStruct((comps, CX * CY, NZ)...  38.5 us
    unnamed x27, local copies, waits for them, and re-layouts  7.31 us

profile of v1, /device:TPU:1, one launch (start us, length us, event | category | flops | bytes accessed | tf_op | source)
XLA Modules:
  0.0 46.5 jit_solution(10069880486072465146)
XLA Ops:
  0.6 0.0 copy-start.10
  0.6 0.0 copy-start.11
  0.7 0.0 copy-start.6
  0.7 0.0 copy-start.7
  0.7 0.0 copy-start.8
  0.7 0.0 copy-start.9
  0.7 0.6 %copy-done.10 = f32[32]{0:T(128)S(1)} copy-done((f32[32]{0:T(128)S(1)}, f32[32]{0:T(128)}, u32[]{:S(2)}) %copy-start.10) | copy-done | bytes 152
  1.3 0.0 copy-done.11
  1.3 0.0 copy-done.6
  1.3 0.0 copy-done.7
  1.4 0.0 copy-done.8
  1.4 0.0 copy-done.9
  1.4 0.0 copy-start
  1.4 0.9 %copy-done = f32[3,8,8,128]{3,2,1,0:T(8,128)S(1)} copy-done((f32[3,8,8,128]{3,2,1,0:T(8,128)S(1)}, f32[3,8,8,128]{3,2,1,0:T(8,128)}, u32[]{:S(2)}) %copy-start) | copy-done | bytes 98328
  2.3 0.0 copy-start.1
  2.3 0.9 %copy-done.1 = f32[3,8,8,128]{3,2,1,0:T(8,128)S(1)} copy-done((f32[3,8,8,128]{3,2,1,0:T(8,128)S(1)}, f32[3,8,8,128]{3,2,1,0:T(8,128)}, u32[]{:S(2)}) %copy-start.1) | copy-done | bytes 98328
  3.2 0.0 copy-start.2
  3.2 0.8 %copy-done.2 = f32[3,2,2048]{2,1,0:T(2,128)S(1)} copy-done((f32[3,2,2048]{2,1,0:T(2,128)S(1)}, f32[3,2,2048]{2,1,0:T(2,128)}, u32[]{:S(2)}) %copy-start.2) | copy-done | bytes 49176
  4.0 0.0 copy-start.3
  4.0 0.8 %copy-done.3 = f32[3,2,2048]{2,1,0:T(2,128)S(1)} copy-done((f32[3,2,2048]{2,1,0:T(2,128)S(1)}, f32[3,2,2048]{2,1,0:T(2,128)}, u32[]{:S(2)}) %copy-start.3) | copy-done | bytes 49176
  4.8 0.0 copy-start.4
  4.8 0.8 %copy-done.4 = s32[8,8,128]{2,1,0:T(8,128)S(1)} copy-done((s32[8,8,128]{2,1,0:T(8,128)S(1)}, s32[8,8,128]{2,1,0:T(8,128)}, u32[]{:S(2)}) %copy-start.4) | copy-done | bytes 32792
  5.5 0.0 copy-start.5
  5.5 0.7 %copy-done.5 = s32[2,2048]{1,0:T(2,128)S(1)} copy-done((s32[2,2048]{1,0:T(2,128)S(1)}, s32[2,2048]{1,0:T(2,128)}, u32[]{:S(2)}) %copy-start.5) | copy-done | bytes 16408
  6.2 38.5 %shard_map.139 = (f32[3,64,128]{2,1,0:T(8,128)S(1)}, f32[3,2,2048]{2,1,0:T(2,128)S(1)}, f32[32]{0:T(128)S(1)}) custom-call(f32[3,64,128]{2,1,0:T(8,128)S(1)} %bitcast.5, f32[3,64,128]{2,1,0:T(8,128)S(1)} %bitcast.6, s32[64,128]{1,0:T(8,128)S(1)} %bitcast.7, f32[4]{0:T(128)S(1)} %copy-done.7, f32[3,2,2048]{2,1,0:T(2,128)S(1)} %copy-done.2, ...), custom_call_target="tpu_custom_call" | custom-call | tf_op jit(solution)/shard_map/pallas_call | solution.py:431
  44.7 0.6 %copy.18 = f32[3,8,8,128]{3,2,1,0:T(8,128)} copy(f32[3,8,8,128]{3,2,1,0:T(8,128)S(1)} %bitcast.4) | data formatting | bytes 196608
  45.4 0.6 %copy.19 = f32[3,2,2048]{2,1,0:T(2,128)} copy(f32[3,2,2048]{2,1,0:T(2,128)S(1)} %get-tuple-element.13) | data formatting | bytes 98304
  46.0 0.5 %copy.20 = f32[32]{0:T(128)} copy(f32[32]{0:T(128)S(1)} %get-tuple-element.14) | data formatting | bytes 256
Async XLA Ops:
  0.6 0.7 %copy-start.10 = (f32[32]{0:T(128)S(1)}, f32[32]{0:T(128)}, u32[]{:S(2)}) copy-start(f32[32]{0:T(128)} %gap.1) | copy-start | bytes 388
  0.6 0.7 %copy-start.11 = (f32[32]{0:T(128)S(1)}, f32[32]{0:T(128)}, u32[]{:S(2)}) copy-start(f32[32]{0:T(128)} %contact.1) | copy-start | bytes 388
  0.7 0.7 %copy-start.6 = (f32[3,32]{1,0:T(4,128)S(1)}, f32[3,32]{1,0:T(4,128)}, u32[]{:S(2)}) copy-start(f32[3,32]{1,0:T(4,128)} %normal.1) | copy-start | bytes 1156
  0.7 0.7 %copy-start.7 = (f32[4]{0:T(128)S(1)}, f32[4]{0:T(128)}, u32[]{:S(2)}) copy-start(f32[4]{0:T(128)} %table.1) | copy-start | bytes 52
  0.7 0.7 %copy-start.8 = (s32[32]{0:T(128)S(1)}, s32[32]{0:T(128)}, u32[]{:S(2)}) copy-start(s32[32]{0:T(128)} %pair_sphere.1) | copy-start | bytes 388
  0.7 0.7 %copy-start.9 = (s32[32]{0:T(128)S(1)}, s32[32]{0:T(128)}, u32[]{:S(2)}) copy-start(s32[32]{0:T(128)} %pair_partner.1) | copy-start | bytes 388
  1.4 0.9 %copy-start = (f32[3,8,8,128]{3,2,1,0:T(8,128)S(1)}, f32[3,8,8,128]{3,2,1,0:T(8,128)}, u32[]{:S(2)}) copy-start(f32[3,8,8,128]{3,2,1,0:T(8,128)} %param.12) | copy-start | bytes 294916
  2.3 0.9 %copy-start.1 = (f32[3,8,8,128]{3,2,1,0:T(8,128)S(1)}, f32[3,8,8,128]{3,2,1,0:T(8,128)}, u32[]{:S(2)}) copy-start(f32[3,8,8,128]{3,2,1,0:T(8,128)} %param.13) | copy-start | bytes 294916
  3.2 0.8 %copy-start.2 = (f32[3,2,2048]{2,1,0:T(2,128)S(1)}, f32[3,2,2048]{2,1,0:T(2,128)}, u32[]{:S(2)}) copy-start(f32[3,2,2048]{2,1,0:T(2,128)} %mult.1) | copy-start | bytes 147460
  4.0 0.8 %copy-start.3 = (f32[3,2,2048]{2,1,0:T(2,128)S(1)}, f32[3,2,2048]{2,1,0:T(2,128)}, u32[]{:S(2)}) copy-start(f32[3,2,2048]{2,1,0:T(2,128)} %frac.1) | copy-start | bytes 147460
  4.8 0.8 %copy-start.4 = (s32[8,8,128]{2,1,0:T(8,128)S(1)}, s32[8,8,128]{2,1,0:T(8,128)}, u32[]{:S(2)}) copy-start(s32[8,8,128]{2,1,0:T(8,128)} %param.14) | copy-start | bytes 98308
  5.5 0.7 %copy-start.5 = (s32[2,2048]{1,0:T(2,128)S(1)}, s32[2,2048]{1,0:T(2,128)}, u32[]{:S(2)}) copy-start(s32[2,2048]{1,0:T(2,128)} %cell.1) | copy-start | bytes 49156

commit v2 on v1

--- a/solution.py
+++ b/solution.py
@@ -12,7 +12,7 @@
 
 CX, CY, NZ = 8, 8, 128
 SPH, MARK = 2, 2048
-CHUNK = 512
+CHUNK = 256
 PER_SPHERE = MARK // CHUNK
 CHUNKS = SPH * PER_SPHERE
 ROWS = 88
@@ -26,6 +26,10 @@
     return (x + 2) * 16 + y % 16
 
 
+def span(direction):
+    return (0, 1, 2) if direction == 1 else (6, 7)
+
+
 def split(value):
     high = value.astype(BF16)
     low = (value - high.astype(F32)).astype(BF16)
@@ -33,11 +37,12 @@
 
 
 def body(
-    vel, force, visc_class, table, mult, cell, frac, pair_sphere, pair_partner, normal, gap, contact,
-    vel_out, mult_out, contact_out,
-    own, ext, pack, halo_in, coef, rhs, grid, grid_pack, grid_diag, grid_in, diag_in,
+    vel_hbm, force_hbm, class_hbm, table_hbm, mult_hbm, cell_hbm, frac_hbm, sphere_hbm, partner_hbm, normal_hbm, gap_hbm,
+    contact_hbm, vel_hbm_out, mult_hbm_out, contact_hbm_out,
+    own, ext, pack, halo_in, halo_diag, halo_diag_in, coef, rhs, grid, grid_pack, grid_diag, grid_in, diag_in,
+    visc_class, table, cell, frac, mult, force, pair_sphere, pair_partner, normal, gap, contact,
     acc, share_acc, share, plane_w, depth_w, stack, left, mult_mid, rigid, rigid_in, normal8, contact_mid,
-    send_sem, recv_sem,
+    vel_out, mult_out, contact_out, load_sem, send_sem, recv_sem,
 ):
     wide, narrow = lax.axis_index("wide"), lax.axis_index("narrow")
     n_wide, n_narrow = lax.axis_size("wide"), lax.axis_size("narrow")
@@ -46,9 +51,32 @@
         dx, dy = d // 3 - 1, d % 3 - 1
         return (lax.rem(wide + dx + n_wide, n_wide), lax.rem(narrow + dy + n_narrow, n_narrow))
 
+    def exists(d):
+        dx, dy = d // 3 - 1, d % 3 - 1
+        return (wide + dx >= 0) & (wide + dx < n_wide) & (narrow + dy >= 0) & (narrow + dy < n_narrow)
+
     barrier = pltpu.get_barrier_semaphore()
     for d in OTHERS:
-        pl.semaphore_signal(barrier, inc=1, device_id=neighbour(d), device_id_type=MESH)
+        @pl.when(exists(d))
+        def greet(d=d):
+            pl.semaphore_signal(barrier, inc=1, device_id=neighbour(d), device_id_type=MESH)
+    across = jnp.where(wide > 0, 1, 0) + jnp.where(wide < n_wide - 1, 1, 0) + 1
+    along = jnp.where(narrow > 0, 1, 0) + jnp.where(narrow < n_narrow - 1, 1, 0) + 1
+
+    loads = [
+        pltpu.make_async_copy(src, dst, load_sem.at[k])
+        for k, (src, dst) in enumerate((
+            (class_hbm, visc_class), (table_hbm, table), (vel_hbm, own.at[0, 0:3]), (cell_hbm, cell), (frac_hbm, frac),
+            (mult_hbm, mult), (force_hbm, force), (sphere_hbm, pair_sphere), (partner_hbm, pair_partner),
+            (normal_hbm, normal), (gap_hbm, gap), (contact_hbm, contact),
+        ))
+    ]
+    for load in loads:
+        load.start()
+    stores = [
+        pltpu.make_async_copy(src, dst, load_sem.at[12 + k])
+        for k, (src, dst) in enumerate(((vel_out, vel_hbm_out), (mult_out, mult_hbm_out), (contact_out, contact_hbm_out)))
+    ]
 
     def transfer(kind, s, src, dst):
         return pltpu.make_async_remote_copy(
@@ -61,10 +89,15 @@
         copies = []
         for s in OTHERS:
             dx, dy = s // 3 - 1, s % 3 - 1
+            if dx != 0 and dy != 0:
+                count = fields * len(span(dx)) * len(span(dy))
+                rows = (count + 7) // 8 * 8
+                copies.append(transfer(HALO0 if turn == 0 else HALO1, s, halo_diag.at[turn, s, 0:rows], halo_diag_in.at[turn, s, 0:rows]))
+                continue
             if dy == 0:
                 rows = 24 if dx == 1 else 16
-                start = 0 if dx == 1 else 48
-                src = own.at[turn, 0:fields, start:start + rows]
+                first = 0 if dx == 1 else 48
+                src = own.at[turn, 0:fields, first:first + rows]
             else:
                 rows = 24 if dy == 1 else 16
                 src = pack.at[turn, 0 if dy == 1 else 1, 0:fields, 0:rows]
@@ -91,16 +124,25 @@
         ]
 
     def start(copies):
-        for copy in copies:
-            copy.start()
+        for s, copy in zip(OTHERS, copies):
+            @pl.when(exists(8 - s))
+            def go(copy=copy):
+                copy.start()
 
     def arrive(copies):
-        for copy in copies:
-            copy.wait_recv()
+        for s, copy in zip(OTHERS, copies):
+            @pl.when(exists(s))
+            def go(copy=copy):
+                copy.wait_recv()
 
     def leave(copies):
-        for copy in copies:
-            copy.wait_send()
+        for s, copy in zip(OTHERS, copies):
+            @pl.when(exists(8 - s))
+            def go(copy=copy):
+                copy.wait_send()
+
+    def received(s, value):
+        return jnp.where(exists(s), value, F32(0.0))
 
     def pack_halo(turn):
         fields = 4 if turn == 0 else 3
@@ -110,36 +152,50 @@
             for j in range(2):
                 pack[turn, 1, f, 8 * j:8 * j + 8, :] = own[turn, f, pl.ds(6 + j, 8, stride=8), :]
 
+        for s in (0, 2, 6, 8):
+            xs, ys = span(s // 3 - 1), span(s % 3 - 1)
+            for f in range(fields):
+                for j, y in enumerate(ys):
+                    at = (f * len(ys) + j) * len(xs)
+                    halo_diag[turn, s, at:at + len(xs), :] = own[turn, f, pl.ds(xs[0] * 8 + y, len(xs), stride=8), :]
+
     def unpack_halo(turn):
         fields = 4 if turn == 0 else 3
         for f in range(fields):
             for i in range(3):
-                ext[turn, f, pl.ds(row(8 + i, 0), 8), :] = halo_in[turn, 7, f, 8 * i:8 * i + 8, :]
+                ext[turn, f, pl.ds(row(8 + i, 0), 8), :] = received(7, halo_in[turn, 7, f, 8 * i:8 * i + 8, :])
             for i in range(2):
-                ext[turn, f, pl.ds(row(i - 2, 0), 8), :] = halo_in[turn, 1, f, 8 * i:8 * i + 8, :]
+                ext[turn, f, pl.ds(row(i - 2, 0), 8), :] = received(1, halo_in[turn, 1, f, 8 * i:8 * i + 8, :])
             for j in range(3):
-                ext[turn, f, pl.ds(row(0, 8 + j), 8, stride=16), :] = halo_in[turn, 5, f, 8 * j:8 * j + 8, :]
-                ext[turn, f, pl.ds(row(8, 8 + j), 3, stride=16), :] = halo_in[turn, 8, f, 8 * j:8 * j + 3, :]
-                ext[turn, f, pl.ds(row(-2, 8 + j), 2, stride=16), :] = halo_in[turn, 2, f, 8 * j + 6:8 * j + 8, :]
+                ext[turn, f, pl.ds(row(0, 8 + j), 8, stride=16), :] = received(5, halo_in[turn, 5, f, 8 * j:8 * j + 8, :])
             for j in range(2):
-                ext[turn, f, pl.ds(row(0, j - 2), 8, stride=16), :] = halo_in[turn, 3, f, 8 * j:8 * j + 8, :]
-                ext[turn, f, pl.ds(row(8, j - 2), 3, stride=16), :] = halo_in[turn, 6, f, 8 * j:8 * j + 3, :]
-                ext[turn, f, pl.ds(row(-2, j - 2), 2, stride=16), :] = halo_in[turn, 0, f, 8 * j + 6:8 * j + 8, :]
-
+                ext[turn, f, pl.ds(row(0, j - 2), 8, stride=16), :] = received(3, halo_in[turn, 3, f, 8 * j:8 * j + 8, :])
+            for s in (0, 2, 6, 8):
+                xs, ys = span(s // 3 - 1), span(s % 3 - 1)
+                x0 = 8 if s // 3 == 2 else -2
+                y0 = 8 if s % 3 == 2 else -2
+                for j in range(len(ys)):
+                    at = (f * len(ys) + j) * len(xs)
+                    ext[turn, f, pl.ds(row(x0, y0 + j), len(xs), stride=16), :] = received(
+                        s, halo_diag_in[turn, s, at:at + len(xs), :]
+                    )
+
+    for load in loads[0:3]:
+        load.wait()
     classes = visc_class[...]
     mu = jnp.where(classes == 0, table[0], jnp.where(classes == 1, table[1], jnp.where(classes == 2, table[2], table[3])))
     mu = jnp.where((classes >= 0) & (classes <= 3), mu, F32(0.0))
     own[0, 3, :, :] = mu
-    for c in range(3):
-        own[0, c, :, :] = vel[c]
     for f in range(4):
         for x in range(8):
             ext[0, f, pl.ds(row(x, 0), 8), :] = own[0, f, 8 * x:8 * x + 8, :]
     pack_halo(0)
 
-    pl.semaphore_wait(barrier, 8)
+    pl.semaphore_wait(barrier, across * along - 1)
     start(halo_copies(0))
 
+    for load in loads[3:]:
+        load.wait()
     acc[...] = jnp.zeros_like(acc)
     share_acc[...] = jnp.zeros_like(share_acc)
 
@@ -182,7 +238,7 @@
         share_acc[s] += result[264:352]
         return carry
 
-    lax.fori_loop(0, CHUNKS, setup, 0)
+    lax.fori_loop(0, CHUNKS, setup, 0, unroll=8)
     for s in range(SPH):
         share[s] = (share_acc[s, :, 0:NZ] + share_acc[s, :, NZ:2 * NZ]) * F32(1.0 / MARK)
 
@@ -262,7 +318,7 @@
         coef[6, at, :] = inverse
         return carry
 
-    lax.fori_loop(0, 11, coefficients, 0)
+    lax.fori_loop(0, 11, coefficients, 0, unroll=True)
     rhs[...] = jnp.zeros_like(rhs)
     stack[...] = jnp.zeros_like(stack)
     normal8[...] = jnp.zeros_like(normal8)
@@ -286,21 +342,21 @@
                 rhs[turn, c, pl.ds(row(x, 0), 8), :] = grid[turn, c, 8 + 8 * x:16 + 8 * x, :]
             rhs[turn, c, pl.ds(row(0, 8), 8, stride=16), :] = grid[turn, c, 0:8, :]
             rhs[turn, c, pl.ds(row(8, 8), 1), :] = grid[turn, c, 81:82, :]
-            add(8, 0, 8, 1, grid_in[turn, 7, c, 8:16, :])
-            add(9, 0, 8, 1, grid_in[turn, 7, c, 16:24, :])
-            add(8, 8, 2, 16, grid_in[turn, 7, c, 0:2, :])
-            add(-1, 0, 8, 1, grid_in[turn, 1, c, 0:8, :])
-            add(0, 0, 8, 1, grid_in[turn, 1, c, 8:16, :])
-            add(-1, 8, 2, 16, grid_in[turn, 1, c, 16:18, :])
+            add(8, 0, 8, 1, received(7, grid_in[turn, 7, c, 8:16, :]))
+            add(9, 0, 8, 1, received(7, grid_in[turn, 7, c, 16:24, :]))
+            add(8, 8, 2, 16, received(7, grid_in[turn, 7, c, 0:2, :]))
+            add(-1, 0, 8, 1, received(1, grid_in[turn, 1, c, 0:8, :]))
+            add(0, 0, 8, 1, received(1, grid_in[turn, 1, c, 8:16, :]))
+            add(-1, 8, 2, 16, received(1, grid_in[turn, 1, c, 16:18, :]))
             for s, low in ((5, 8), (3, -1)):
                 for j in range(2):
-                    add(0, low + j, 8, 16, grid_in[turn, s, c, 8 * j:8 * j + 8, :])
-                    add(8, low + j, 1, 1, grid_in[turn, s, c, 16 + j:17 + j, :])
+                    add(0, low + j, 8, 16, received(s, grid_in[turn, s, c, 8 * j:8 * j + 8, :]))
+                    add(8, low + j, 1, 1, received(s, grid_in[turn, s, c, 16 + j:17 + j, :]))
             for s in (0, 2, 6, 8):
                 x = 8 if s // 3 == 2 else -1
                 y = 8 if s % 3 == 2 else -1
                 for j in range(2):
-                    add(x, y + j, 2, 16, diag_in[turn, s, 4 * c + 2 * j:4 * c + 2 * j + 2, :])
+                    add(x, y + j, 2, 16, received(s, diag_in[turn, s, 4 * c + 2 * j:4 * c + 2 * j + 2, :]))
 
     def sweep(source, target, first, count, turn):
         def one(i, carry):
@@ -321,7 +377,7 @@
                 target[c, pl.ds(pl.multiple_of((i + 1) * 16, 16), 16), :] = value
             return carry
 
-        lax.fori_loop(first, first + count, one, 0)
+        lax.fori_loop(first, first + count, one, 0, unroll=True)
 
     def update_contact(turn):
         quarter = pair_q // 2
@@ -330,9 +386,7 @@
             if q == 4:
                 tile = rigid[turn, :, 0:32]
             else:
-                qx, qy = q // 3 - 1, q % 3 - 1
-                inside = (wide + qx >= 0) & (wide + qx < n_wide) & (narrow + qy >= 0) & (narrow + qy < n_narrow)
-                tile = jnp.where(inside, rigid_in[turn, q, :, 0:32], F32(0.0))
+                tile = received(q, rigid_in[turn, q, :, 0:32])
             partner = jnp.where(quarter == q, tile, partner)
         closing8 = jnp.where(sphere_row == pair_q - 2 * quarter, partner, F32(0.0)) - jnp.where(
             sphere_row == pair_s, rigid[turn, :, 0:32], F32(0.0)
@@ -368,6 +422,8 @@
         if turn > 0:
             arrive(rigid_copies(turn - 1))
             contact_mid[...] = update_contact(turn - 1)
+        if last:
+            stores[0].start()
         sums = jnp.zeros((8, NZ), F32)
         row8 = lax.broadcasted_iota(jnp.int32, (8, NZ), 0)
         for s in range(SPH):
@@ -391,12 +447,12 @@
             s, k = n // PER_SPHERE, n % PER_SPHERE
             lanes = pl.ds(pl.multiple_of(k * CHUNK, CHUNK), CHUNK)
             weight = plane_w[n]
-            sampled = jnp.dot(left[...], depth_w[n], preferred_element_type=F32)
+            sampled = jnp.dot(left[0:PAD], depth_w[n], preferred_element_type=F32) + jnp.dot(left[PAD:2 * PAD], depth_w[n], preferred_element_type=F32)
             lhs = []
             for c in range(3):
                 rows = slice(c * ROWS, (c + 1) * ROWS)
                 low_rows = slice(PAD + c * ROWS, PAD + (c + 1) * ROWS)
-                read = jnp.sum((sampled[rows] + sampled[low_rows]) * weight, axis=0, keepdims=True)
+                read = jnp.sum(sampled[rows] * weight, axis=0, keepdims=True)
                 speed = rigid[turn, pl.ds(4 * s + c, 1), 0:1]
                 new = source[c, pl.ds(s, 1), lanes] + 0.5 * (speed - read)
                 if last:
@@ -409,15 +465,30 @@
                 acc[...] += add_spread(jnp.concatenate(lhs, axis=0), depth_w[n])
             return carry
 
-        lax.fori_loop(0, CHUNKS, markers, 0)
+        lax.fori_loop(0, CHUNKS, markers, 0, unroll=8)
         if not last:
             send_force(turn + 1)
+    stores[1].start()
     arrive(rigid_copies(ITERS - 1))
     contact_out[...] = update_contact(ITERS - 1).reshape(32)
+    stores[2].start()
     for turn in range(ITERS):
         leave(halo_copies(turn))
         leave(force_copies(turn))
         leave(rigid_copies(turn))
+    for store in stores:
+        store.wait()
+
+
+def hand_over(vel, mult, contact, vel_out, mult_out, contact_out, sem):
+    copies = [
+        pltpu.make_async_copy(src, dst, sem.at[k])
+        for k, (src, dst) in enumerate(((vel, vel_out), (mult, mult_out), (contact, contact_out)))
+    ]
+    for copy in copies:
+        copy.start()
+    for copy in copies:
+        copy.wait()
 
 
 def local(
@@ -425,23 +496,24 @@
     pair_sphere, pair_partner, pair_normal, pair_gap, contact_force,
 ):
     comps = 3
-    vmem = pl.BlockSpec(memory_space=pltpu.VMEM)
-    specs = [vmem] * 12
-    specs[3] = pl.BlockSpec(memory_space=pltpu.SMEM)
+    hbm = pl.BlockSpec(memory_space=pltpu.MemorySpace.HBM)
+    out_shape = (
+        jax.ShapeDtypeStruct((comps, CX * CY, NZ), F32),
+        jax.ShapeDtypeStruct(multiplier.shape, F32),
+        jax.ShapeDtypeStruct(contact_force.shape, F32),
+    )
     out = pl.pallas_call(
         body,
-        out_shape=(
-            jax.ShapeDtypeStruct((comps, CX * CY, NZ), F32),
-            jax.ShapeDtypeStruct(multiplier.shape, F32),
-            jax.ShapeDtypeStruct(contact_force.shape, F32),
-        ),
-        in_specs=specs,
-        out_specs=(vmem, vmem, vmem),
+        out_shape=out_shape,
+        in_specs=[hbm] * 12,
+        out_specs=(hbm, hbm, hbm),
         scratch_shapes=[
             pltpu.VMEM((2, 4, CX * CY, NZ), F32),
             pltpu.VMEM((4, 4, EXT, NZ), F32),
             pltpu.VMEM((2, 2, 4, 24, NZ), F32),
             pltpu.VMEM((2, 9, 4, 24, NZ), F32),
+            pltpu.VMEM((2, 9, 40, NZ), F32),
+            pltpu.VMEM((2, 9, 40, NZ), F32),
             pltpu.VMEM((7, 11 * 16, NZ), F32),
             pltpu.VMEM((2, comps, EXT, NZ), F32),
             pltpu.VMEM((2, comps, ROWS, NZ), F32),
@@ -449,6 +521,17 @@
             pltpu.VMEM((2, 9, 16, NZ), F32),
             pltpu.VMEM((2, 9, comps, 24, NZ), F32),
             pltpu.VMEM((2, 9, 16, NZ), F32),
+            pltpu.VMEM((CX * CY, NZ), jnp.int32),
+            pltpu.SMEM(visc_table.shape, F32),
+            pltpu.VMEM(marker_cell.shape, jnp.int32),
+            pltpu.VMEM(marker_frac.shape, F32),
+            pltpu.VMEM(multiplier.shape, F32),
+            pltpu.VMEM((comps, CX * CY, NZ), F32),
+            pltpu.VMEM(pair_sphere.shape, jnp.int32),
+            pltpu.VMEM(pair_partner.shape, jnp.int32),
+            pltpu.VMEM(pair_normal.shape, F32),
+            pltpu.VMEM(pair_gap.shape, F32),
+            pltpu.VMEM(contact_force.shape, F32),
             pltpu.VMEM((PAD, 2 * NZ), F32),
             pltpu.VMEM((SPH, ROWS, 2 * NZ), F32),
             pltpu.VMEM((SPH, ROWS, NZ), F32),
@@ -461,16 +544,28 @@
             pltpu.VMEM((2, 9, 8, NZ), F32),
             pltpu.VMEM((8, 32), F32),
             pltpu.VMEM((1, 32), F32),
+            pltpu.VMEM((comps, CX * CY, NZ), F32),
+            pltpu.VMEM(multiplier.shape, F32),
+            pltpu.VMEM(contact_force.shape, F32),
+            pltpu.SemaphoreType.DMA((15,)),
             pltpu.SemaphoreType.DMA((6, 9)),
             pltpu.SemaphoreType.DMA((6, 9)),
         ],
         compiler_params=pltpu.CompilerParams(
-            collective_id=0, has_side_effects=True, vmem_limit_bytes=48 * 1024 * 1024
+            collective_id=0, has_side_effects=True, vmem_limit_bytes=63 * 1024 * 1024
         ),
     )(
         velocity.reshape(comps, CX * CY, NZ), force.reshape(comps, CX * CY, NZ), visc_class.reshape(CX * CY, NZ),
         visc_table, multiplier, marker_cell, marker_frac, pair_sphere, pair_partner, pair_normal, pair_gap, contact_force,
     )
+    out = pl.pallas_call(
+        hand_over,
+        out_shape=out_shape,
+        in_specs=[hbm] * 3,
+        out_specs=(hbm, hbm, hbm),
+        scratch_shapes=[pltpu.SemaphoreType.DMA((3,))],
+        compiler_params=pltpu.CompilerParams(vmem_limit_bytes=63 * 1024 * 1024),
+    )(*out)
     return (out[0].reshape(comps, CX, CY, NZ), out[1], out[2])
 
 

time: 46.9 us -> 33.8 us (0.72)
  the two profiles are of different devices: /device:TPU:1 before, /device:TPU:31 now
where the time goes in v2:
time: 33.8 us; the launch traced here: 33.7 us
  Pallas kernels  33 us (98%)
  between operations  0.64 us (2%)
    pallas_call x1, Pallas kernels, local(): pl.pallas_call(body, out_shape=out_shape, in_specs=[hbm] * 12, out_specs=...  27.4 us
    pallas_call x1, Pallas kernels, local(): pl.pallas_call(hand_over, out_shape=out_shape, in_specs=[hbm] * 3, out_sp...  5.61 us

profile of v2, /device:TPU:31, one launch (start us, length us, event | category | flops | bytes accessed | tf_op | source)
XLA Modules:
  0.0 33.7 jit_solution(14687117284563189297)
XLA Ops:
  0.6 27.4 %shard_map.139 = (f32[3,64,128]{2,1,0:T(8,128)}, f32[3,2,2048]{2,1,0:T(2,128)}, f32[32]{0:T(128)}) custom-call(f32[3,64,128]{2,1,0:T(8,128)} %bitcast.4, f32[3,64,128]{2,1,0:T(8,128)} %bitcast.5, s32[64,128]{1,0:T(8,128)} %bitcast.6, f32[4]{0:T(128)} %table_hbm.1, f32[3,2,2048]{2,1,0:T(2,128)} %mult_hbm.1, s32[2,2048]{1,0:T(2,128)} %cell_hbm.1, ...), custom_call_target="tpu_custom_call" | custom-call | tf_op jit(solution)/shard_map/pallas_call | solution.py:505
  28.0 5.6 %shard_map.140 = (f32[3,64,128]{2,1,0:T(8,128)}, f32[3,2,2048]{2,1,0:T(2,128)}, f32[32]{0:T(128)}) custom-call(f32[3,64,128]{2,1,0:T(8,128)} %get-tuple-element.9.vel, f32[3,2,2048]{2,1,0:T(2,128)} %get-tuple-element.10.mult, f32[32]{0:T(128)} %get-tuple-element.11.contact), custom_call_target="tpu_custom_call" | custom-call | tf_op jit(solution)/shard_map/pallas_call | solution.py:561

commit v3 on v2

--- a/solution.py
+++ b/solution.py
@@ -38,11 +38,11 @@
 
 def body(
     vel_hbm, force_hbm, class_hbm, table_hbm, mult_hbm, cell_hbm, frac_hbm, sphere_hbm, partner_hbm, normal_hbm, gap_hbm,
-    contact_hbm, vel_hbm_out, mult_hbm_out, contact_hbm_out,
+    contact_hbm, vel_out, mult_out, contact_out,
     own, ext, pack, halo_in, halo_diag, halo_diag_in, coef, rhs, grid, grid_pack, grid_diag, grid_in, diag_in,
     visc_class, table, cell, frac, mult, force, pair_sphere, pair_partner, normal, gap, contact,
     acc, share_acc, share, plane_w, depth_w, stack, left, mult_mid, rigid, rigid_in, normal8, contact_mid,
-    vel_out, mult_out, contact_out, load_sem, send_sem, recv_sem,
+    load_sem, send_sem, recv_sem,
 ):
     wide, narrow = lax.axis_index("wide"), lax.axis_index("narrow")
     n_wide, n_narrow = lax.axis_size("wide"), lax.axis_size("narrow")
@@ -73,10 +73,6 @@
     ]
     for load in loads:
         load.start()
-    stores = [
-        pltpu.make_async_copy(src, dst, load_sem.at[12 + k])
-        for k, (src, dst) in enumerate(((vel_out, vel_hbm_out), (mult_out, mult_hbm_out), (contact_out, contact_hbm_out)))
-    ]
 
     def transfer(kind, s, src, dst):
         return pltpu.make_async_remote_copy(
@@ -422,8 +418,6 @@
         if turn > 0:
             arrive(rigid_copies(turn - 1))
             contact_mid[...] = update_contact(turn - 1)
-        if last:
-            stores[0].start()
         sums = jnp.zeros((8, NZ), F32)
         row8 = lax.broadcasted_iota(jnp.int32, (8, NZ), 0)
         for s in range(SPH):
@@ -468,16 +462,12 @@
         lax.fori_loop(0, CHUNKS, markers, 0, unroll=8)
         if not last:
             send_force(turn + 1)
-    stores[1].start()
     arrive(rigid_copies(ITERS - 1))
     contact_out[...] = update_contact(ITERS - 1).reshape(32)
-    stores[2].start()
     for turn in range(ITERS):
         leave(halo_copies(turn))
         leave(force_copies(turn))
         leave(rigid_copies(turn))
-    for store in stores:
-        store.wait()
 
 
 def hand_over(vel, mult, contact, vel_out, mult_out, contact_out, sem):
@@ -496,6 +486,7 @@
     pair_sphere, pair_partner, pair_normal, pair_gap, contact_force,
 ):
     comps = 3
+    vmem = pl.BlockSpec(memory_space=pltpu.VMEM)
     hbm = pl.BlockSpec(memory_space=pltpu.MemorySpace.HBM)
     out_shape = (
         jax.ShapeDtypeStruct((comps, CX * CY, NZ), F32),
@@ -504,9 +495,9 @@
     )
     out = pl.pallas_call(
         body,
-        out_shape=out_shape,
+        out_shape=tuple(pltpu.VMEM(shape.shape, shape.dtype) for shape in out_shape),
         in_specs=[hbm] * 12,
-        out_specs=(hbm, hbm, hbm),
+        out_specs=(vmem, vmem, vmem),
         scratch_shapes=[
             pltpu.VMEM((2, 4, CX * CY, NZ), F32),
             pltpu.VMEM((4, 4, EXT, NZ), F32),
@@ -544,15 +535,12 @@
             pltpu.VMEM((2, 9, 8, NZ), F32),
             pltpu.VMEM((8, 32), F32),
             pltpu.VMEM((1, 32), F32),
-            pltpu.VMEM((comps, CX * CY, NZ), F32),
-            pltpu.VMEM(multiplier.shape, F32),
-            pltpu.VMEM(contact_force.shape, F32),
-            pltpu.SemaphoreType.DMA((15,)),
+            pltpu.SemaphoreType.DMA((12,)),
             pltpu.SemaphoreType.DMA((6, 9)),
             pltpu.SemaphoreType.DMA((6, 9)),
         ],
         compiler_params=pltpu.CompilerParams(
-            collective_id=0, has_side_effects=True, vmem_limit_bytes=63 * 1024 * 1024
+            collective_id=0, has_side_effects=True, vmem_limit_bytes=62 * 1024 * 1024
         ),
     )(
         velocity.reshape(comps, CX * CY, NZ), force.reshape(comps, CX * CY, NZ), visc_class.reshape(CX * CY, NZ),
@@ -561,10 +549,10 @@
     out = pl.pallas_call(
         hand_over,
         out_shape=out_shape,
-        in_specs=[hbm] * 3,
+        in_specs=[vmem] * 3,
         out_specs=(hbm, hbm, hbm),
         scratch_shapes=[pltpu.SemaphoreType.DMA((3,))],
-        compiler_params=pltpu.CompilerParams(vmem_limit_bytes=63 * 1024 * 1024),
+        compiler_params=pltpu.CompilerParams(vmem_limit_bytes=1024 * 1024),
     )(*out)
     return (out[0].reshape(comps, CX, CY, NZ), out[1], out[2])
 

time: 33.8 us -> 28.4 us (0.84)
  Pallas kernels: 33 us -> 27.6 us
    pallas_call x2, Pallas kernels: 33 us -> 27.6 us  [the longest x1 26.9 us: local(): pl.pallas_call(body, out_shape=tuple((pltpu.VMEM(shape.shape, shape.dtype...]
where the time goes in v3:
time: 28.4 us; the launch traced here: 28.2 us
  Pallas kernels  27.6 us (97%)
  between operations  0.64 us (2%)
    pallas_call x1, Pallas kernels, local(): pl.pallas_call(body, out_shape=tuple((pltpu.VMEM(shape.shape, shape.dtype...  26.9 us
    pallas_call x1, Pallas kernels, local(): pl.pallas_call(hand_over, out_shape=out_shape, in_specs=[vmem] * 3, out_s...  0.68 us

profile of v3, /device:TPU:31, one launch (start us, length us, event | category | flops | bytes accessed | tf_op | source)
XLA Modules:
  0.0 28.2 jit_solution(5517249326356722913)
XLA Ops:
  0.6 26.9 %shard_map.139 = (f32[3,64,128]{2,1,0:T(8,128)S(1)}, f32[3,2,2048]{2,1,0:T(2,128)S(1)}, f32[32]{0:T(128)S(1)}) custom-call(f32[3,64,128]{2,1,0:T(8,128)} %bitcast.4, f32[3,64,128]{2,1,0:T(8,128)} %bitcast.5, s32[64,128]{1,0:T(8,128)} %bitcast.6, f32[4]{0:T(128)} %table_hbm.1, f32[3,2,2048]{2,1,0:T(2,128)} %mult_hbm.1, s32[2,2048]{1,0:T(2,128)} %cell_hbm.1, ...), custom_call_target="tpu_custom_call" | custom-call | tf_op jit(solution)/shard_map/pallas_call | solution.py:496
  27.6 0.7 %shard_map.140 = (f32[3,64,128]{2,1,0:T(8,128)}, f32[3,2,2048]{2,1,0:T(2,128)}, f32[32]{0:T(128)}) custom-call(f32[3,64,128]{2,1,0:T(8,128)S(1)} %get-tuple-element.9.vel, f32[3,2,2048]{2,1,0:T(2,128)S(1)} %get-tuple-element.10.mult, f32[32]{0:T(128)S(1)} %get-tuple-element.11.contact), custom_call_target="tpu_custom_call" | custom-call | tf_op jit(solution)/shard_map/pallas_call | solution.py:549

commit v4 on v3

--- a/solution.py
+++ b/solution.py
@@ -19,7 +19,7 @@
 PAD = 272
 EXT = 13 * 16
 HALO0, FORCE0, HALO1, FORCE1, RIGID0, RIGID1 = range(6)
-OTHERS = [0, 1, 2, 3, 5, 6, 7, 8]
+OTHERS = [3, 5, 0, 2, 6, 8, 1, 7]
 
 
 def row(x, y):
@@ -106,11 +106,8 @@
             dx, dy = s // 3 - 1, s % 3 - 1
             if dx != 0 and dy != 0:
                 src, dst = grid_diag.at[turn, s], diag_in.at[turn, s]
-            elif dy == 0:
-                start = 0 if dx == 1 else 64
-                src, dst = grid.at[turn, :, start:start + 24], grid_in.at[turn, s]
             else:
-                src, dst = grid_pack.at[turn, 0 if dy == 1 else 1], grid_in.at[turn, s]
+                src, dst = grid_pack.at[turn, s], grid_in.at[turn, s]
             copies.append(transfer(FORCE0 if turn == 0 else FORCE1, s, src, dst))
         return copies
 
@@ -186,9 +183,6 @@
         for x in range(8):
             ext[0, f, pl.ds(row(x, 0), 8), :] = own[0, f, 8 * x:8 * x + 8, :]
     pack_halo(0)
-
-    pl.semaphore_wait(barrier, across * along - 1)
-    start(halo_copies(0))
 
     for load in loads[3:]:
         load.wait()
@@ -229,15 +223,21 @@
         weight = jnp.concatenate(tiles, axis=0)
         plane_w[n] = weight
         lhs = [weight * (0.25 * mult[c, pl.ds(s, 1), lanes]) for c in range(3)]
-        result = add_spread(jnp.concatenate(lhs + [weight], axis=0), depth_w[n])
-        acc[0:264, :] += result[0:264]
-        share_acc[s] += result[264:352]
+        lhs.append(jnp.zeros((8, CHUNK), F32))
+        acc[...] += add_spread(jnp.concatenate(lhs, axis=0), depth_w[n])
         return carry
 
-    lax.fori_loop(0, CHUNKS, setup, 0, unroll=8)
-    for s in range(SPH):
-        share[s] = (share_acc[s, :, 0:NZ] + share_acc[s, :, NZ:2 * NZ]) * F32(1.0 / MARK)
-
+    def part(h, carry):
+        lax.fori_loop(0, CHUNKS // 2, lambda k, none: setup(h * (CHUNKS // 2) + k, none), 0, unroll=8)
+
+        @pl.when(h == 0)
+        def meet():
+            pl.semaphore_wait(barrier, across * along - 1)
+            start(halo_copies(0))
+
+        return carry
+
+    lax.fori_loop(0, 2, part, 0)
     def send_force(turn):
         for c in range(3):
             base = c * ROWS
@@ -246,13 +246,16 @@
                 if 1 <= t <= 8:
                     part = part + force[c, 8 * t - 8:8 * t, :]
                 grid[turn, c, 8 * t:8 * t + 8, :] = part
-            for j in range(2):
-                grid_pack[turn, 0, c, 8 * j:8 * j + 8, :] = grid[turn, c, pl.ds(8 + j, 8, stride=8), :]
-            grid_pack[turn, 0, c, 16:24, :] = grid[turn, c, 72:80, :]
-            grid_pack[turn, 1, c, 0:8, :] = grid[turn, c, pl.ds(15, 8, stride=8), :]
-            grid_pack[turn, 1, c, 8:16, :] = grid[turn, c, 0:8, :]
-            grid_pack[turn, 1, c, 16:17, :] = grid[turn, c, 79:80, :]
-            grid_pack[turn, 1, c, 17:18, :] = grid[turn, c, 81:82, :]
+        for s, tiles, extra in (
+            (5, (pl.ds(8, 8, stride=8), pl.ds(9, 8, stride=8)), (72, 73)),
+            (3, (pl.ds(15, 8, stride=8), pl.ds(0, 8)), (79, 81)),
+        ):
+            for c in range(3):
+                for j in range(2):
+                    grid_pack[turn, s, 16 * c + 8 * j:16 * c + 8 * j + 8, :] = grid[turn, c, tiles[j], :]
+                    at = 48 + 2 * c + j
+                    grid_pack[turn, s, at:at + 1, :] = grid[turn, c, extra[j]:extra[j] + 1, :]
+        for c in range(3):
             for s in (0, 2, 6, 8):
                 dx, dy = s // 3 - 1, s % 3 - 1
                 first = 8 if dx == 1 else 64
@@ -265,9 +268,36 @@
                         at = 0 if dx == 1 else 80
                         rows = grid[turn, c, at:at + 2, :]
                     grid_diag[turn, s, 4 * c + 2 * j:4 * c + 2 * j + 2, :] = rows
+        for s, first, extra in ((7, 8, 0), (1, 64, 80)):
+            for c in range(3):
+                grid_pack[turn, s, 16 * c:16 * c + 16, :] = grid[turn, c, first:first + 16, :]
+                grid_pack[turn, s, 48 + 2 * c:50 + 2 * c, :] = grid[turn, c, extra:extra + 2, :]
         start(force_copies(turn))
 
     send_force(0)
+
+    def shares(n, carry):
+        pad = jnp.zeros((8, CHUNK), F32)
+        for s in range(SPH):
+            lhs = jnp.concatenate([plane_w[s * PER_SPHERE + n], pad], axis=0)
+            share_acc[s] += add_spread(lhs, depth_w[s * PER_SPHERE + n])
+        return carry
+
+    lax.fori_loop(0, PER_SPHERE, shares, 0, unroll=4)
+    for s in range(SPH):
+        share[s] = (share_acc[s, 0:ROWS, 0:NZ] + share_acc[s, 0:ROWS, NZ:2 * NZ]) * F32(1.0 / MARK)
+
+    rhs[...] = jnp.zeros_like(rhs)
+    stack[...] = jnp.zeros_like(stack)
+    normal8[...] = jnp.zeros_like(normal8)
+    normal8[0:3, :] = normal[...]
+    normal8[4:7, :] = normal[...]
+
+    sphere_row = lax.broadcasted_iota(jnp.int32, (8, 32), 0) // 4
+    pair_s = pair_sphere[...].reshape(1, 32)
+    pair_q = pair_partner[...].reshape(1, 32)
+    contact_mid[...] = contact[...].reshape(1, 32)
+    pair_gap = gap[...].reshape(1, 32)
 
     halos = halo_copies(0)
     arrive(halos)
@@ -315,65 +345,85 @@
         return carry
 
     lax.fori_loop(0, 11, coefficients, 0, unroll=True)
-    rhs[...] = jnp.zeros_like(rhs)
-    stack[...] = jnp.zeros_like(stack)
-    normal8[...] = jnp.zeros_like(normal8)
-    normal8[0:3, :] = normal[...]
-    normal8[4:7, :] = normal[...]
-
-    sphere_row = lax.broadcasted_iota(jnp.int32, (8, 32), 0) // 4
-    pair_s = pair_sphere[...].reshape(1, 32)
-    pair_q = pair_partner[...].reshape(1, 32)
-    contact_mid[...] = contact[...].reshape(1, 32)
-    pair_gap = gap[...].reshape(1, 32)
-
-    def gather_force(turn):
-        arrive(force_copies(turn))
+    def own_force(turn):
         for c in range(3):
-            def add(x, y, n, stride, value):
-                at = pl.ds(row(x, y), n, stride=stride) if stride != 1 else pl.ds(row(x, y), n)
-                rhs[turn, c, at, :] += value
-
             for x in range(9):
                 rhs[turn, c, pl.ds(row(x, 0), 8), :] = grid[turn, c, 8 + 8 * x:16 + 8 * x, :]
             rhs[turn, c, pl.ds(row(0, 8), 8, stride=16), :] = grid[turn, c, 0:8, :]
             rhs[turn, c, pl.ds(row(8, 8), 1), :] = grid[turn, c, 81:82, :]
-            add(8, 0, 8, 1, received(7, grid_in[turn, 7, c, 8:16, :]))
-            add(9, 0, 8, 1, received(7, grid_in[turn, 7, c, 16:24, :]))
-            add(8, 8, 2, 16, received(7, grid_in[turn, 7, c, 0:2, :]))
-            add(-1, 0, 8, 1, received(1, grid_in[turn, 1, c, 0:8, :]))
-            add(0, 0, 8, 1, received(1, grid_in[turn, 1, c, 8:16, :]))
-            add(-1, 8, 2, 16, received(1, grid_in[turn, 1, c, 16:18, :]))
-            for s, low in ((5, 8), (3, -1)):
-                for j in range(2):
-                    add(0, low + j, 8, 16, received(s, grid_in[turn, s, c, 8 * j:8 * j + 8, :]))
-                    add(8, low + j, 1, 1, received(s, grid_in[turn, s, c, 16 + j:17 + j, :]))
-            for s in (0, 2, 6, 8):
-                x = 8 if s // 3 == 2 else -1
-                y = 8 if s % 3 == 2 else -1
-                for j in range(2):
-                    add(x, y + j, 2, 16, received(s, diag_in[turn, s, 4 * c + 2 * j:4 * c + 2 * j + 2, :]))
-
-    def sweep(source, target, first, count, turn):
+
+    def gather_force(turn):
+        def add(c, x, y, n, stride, s, value):
+            at = pl.ds(row(x, y), n, stride=stride) if stride != 1 else pl.ds(row(x, y), n)
+            rhs[turn, c, at, :] += received(s, value)
+
+        copies = dict(zip(OTHERS, force_copies(turn)))
+        for s in (7, 1, 5, 3, 0, 2, 6, 8):
+            @pl.when(exists(s))
+            def go(copy=copies[s]):
+                copy.wait_recv()
+            x = 8 if s // 3 == 2 else -1
+            y = 8 if s % 3 == 2 else -1
+            for c in range(3):
+                if s in (1, 3, 5, 7):
+                    tile = [grid_in[turn, s, 16 * c + 8 * j:16 * c + 8 * j + 8, :] for j in range(2)]
+                    extra = grid_in[turn, s, 48 + 2 * c:50 + 2 * c, :]
+                if s in (1, 7):
+                    add(c, x, 0, 8, 1, s, tile[0])
+                    add(c, x + 1, 0, 8, 1, s, tile[1])
+                    add(c, x, 8, 2, 16, s, extra)
+                elif s in (3, 5):
+                    for j in range(2):
+                        add(c, 0, y + j, 8, 16, s, tile[j])
+                        add(c, 8, y + j, 1, 1, s, extra[j:j + 1])
+                else:
+                    for j in range(2):
+                        at = 4 * c + 2 * j
+                        add(c, x, y + j, 2, 16, s, diag_in[turn, s, at:at + 2, :])
+
+    def neighbours(source, c, i, factors):
+        def load(shift):
+            return source[c, pl.ds(pl.multiple_of((i + 1 + shift) * 16, 16), 16), :]
+
+        mid = load(0)
+        value = factors[0] * load(-1) + factors[1] * load(1)
+        value += factors[2] * pltpu.roll(mid, 1, 0) + factors[3] * pltpu.roll(mid, 15, 0)
+        return value + (factors[4] * pltpu.roll(mid, 1, 1) + factors[5] * pltpu.roll(mid, NZ - 1, 1))
+
+    def tiles(i):
+        return pl.ds(pl.multiple_of(i * 16, 16), 16), pl.ds(pl.multiple_of((i + 1) * 16, 16), 16)
+
+    def first_sweep(source, target):
         def one(i, carry):
-            at = pl.ds(pl.multiple_of(i * 16, 16), 16)
-            factors = [coef[a, at, :] for a in range(7)]
-            for c in range(3):
-                def load(shift):
-                    return source[c, pl.ds(pl.multiple_of((i + 1 + shift) * 16, 16), 16), :]
-
-                mid = load(0)
-                value = factors[6] * rhs[turn, c, pl.ds(pl.multiple_of((i + 1) * 16, 16), 16), :]
-                value += factors[0] * load(-1)
-                value += factors[1] * load(1)
-                value += factors[2] * pltpu.roll(mid, 1, 0)
-                value += factors[3] * pltpu.roll(mid, 15, 0)
-                value += factors[4] * pltpu.roll(mid, 1, 1)
-                value += factors[5] * pltpu.roll(mid, NZ - 1, 1)
-                target[c, pl.ds(pl.multiple_of((i + 1) * 16, 16), 16), :] = value
+            at, to = tiles(i)
+            factors = [coef[a, at, :] for a in range(6)]
+            for c in range(3):
+                target[c, to, :] = neighbours(source, c, i, factors)
             return carry
 
-        lax.fori_loop(first, first + count, one, 0, unroll=True)
+        lax.fori_loop(0, 11, one, 0, unroll=True)
+
+    def add_force(target, turn):
+        def one(i, carry):
+            at, to = tiles(i)
+            inverse = coef[6, at, :]
+            for c in range(3):
+                value = inverse * rhs[turn, c, to, :]
+                rhs[turn, c, to, :] = value
+                target[c, to, :] += value
+            return carry
+
+        lax.fori_loop(0, 11, one, 0, unroll=True)
+
+    def second_sweep(source, target, turn):
+        def one(i, carry):
+            at, to = tiles(i)
+            factors = [coef[a, at, :] for a in range(6)]
+            for c in range(3):
+                target[c, to, :] = rhs[turn, c, to, :] + neighbours(source, c, i, factors)
+            return carry
+
+        lax.fori_loop(1, 10, one, 0, unroll=True)
 
     def update_contact(turn):
         quarter = pair_q // 2
@@ -395,11 +445,17 @@
         if turn > 0:
             arrive(halo_copies(turn))
             unpack_halo(turn)
+        own_force(turn)
+        middle, done = ext.at[2], ext.at[3]
+        first_sweep(ext.at[turn], middle)
+        if turn > 0:
+            arrive(rigid_copies(turn - 1))
+            contact_mid[...] = update_contact(turn - 1)
+        push = jnp.where(sphere_row == pair_s, normal8[...] * contact_mid[...], F32(0.0))
+        push_sum = 0.5 * jnp.sum(push, axis=1, keepdims=True)
         gather_force(turn)
-        middle = ext.at[2]
-        sweep(ext.at[turn], middle, 0, 11, turn)
-        sweep(middle, ext.at[3], 1, 9, turn)
-        done = ext.at[3]
+        add_force(middle, turn)
+        second_sweep(middle, done, turn)
         for c in range(3):
             for x in range(9):
                 tile = done[c, pl.ds(row(x, 0), 8), :]
@@ -412,21 +468,17 @@
                         ext[turn + 1, c, pl.ds(row(x, 0), 8), :] = tile
             stack[c * ROWS:c * ROWS + 8, :] = done[c, pl.ds(row(0, 8), 8, stride=16), :]
             stack[c * ROWS + 81:c * ROWS + 82, :] = done[c, pl.ds(row(8, 8), 1), :]
+        sums = jnp.zeros((8, NZ), F32)
+        row8 = lax.broadcasted_iota(jnp.int32, (8, NZ), 0)
+        for s in range(SPH):
+            for c in range(3):
+                part = jnp.sum(share[s] * stack[c * ROWS:(c + 1) * ROWS, :], axis=0, keepdims=True)
+                sums = jnp.where(row8 == 4 * s + c, part, sums)
+        speed = jnp.sum(sums, axis=1, keepdims=True) + push_sum
+        rigid[turn] = jnp.broadcast_to(speed, (8, NZ))
         if not last:
             pack_halo(turn + 1)
             start(halo_copies(turn + 1))
-        if turn > 0:
-            arrive(rigid_copies(turn - 1))
-            contact_mid[...] = update_contact(turn - 1)
-        sums = jnp.zeros((8, NZ), F32)
-        row8 = lax.broadcasted_iota(jnp.int32, (8, NZ), 0)
-        for s in range(SPH):
-            for c in range(3):
-                part = jnp.sum(share[s] * stack[c * ROWS:(c + 1) * ROWS, :], axis=0, keepdims=True)
-                sums = jnp.where(row8 == 4 * s + c, part, sums)
-        push = jnp.where(sphere_row == pair_s, normal8[...] * contact_mid[...], F32(0.0))
-        speed = jnp.sum(sums, axis=1, keepdims=True) + 0.5 * jnp.sum(push, axis=1, keepdims=True)
-        rigid[turn] = jnp.broadcast_to(speed, (8, NZ))
         start(rigid_copies(turn))
         high, low = split(stack[...])
         left[0:PAD, 0:NZ] = high
@@ -462,12 +514,13 @@
         lax.fori_loop(0, CHUNKS, markers, 0, unroll=8)
         if not last:
             send_force(turn + 1)
-    arrive(rigid_copies(ITERS - 1))
-    contact_out[...] = update_contact(ITERS - 1).reshape(32)
     for turn in range(ITERS):
         leave(halo_copies(turn))
         leave(force_copies(turn))
-        leave(rigid_copies(turn))
+    leave(rigid_copies(0))
+    arrive(rigid_copies(ITERS - 1))
+    contact_out[...] = update_contact(ITERS - 1).reshape(32)
+    leave(rigid_copies(ITERS - 1))
 
 
 def hand_over(vel, mult, contact, vel_out, mult_out, contact_out, sem):
@@ -508,9 +561,9 @@
             pltpu.VMEM((7, 11 * 16, NZ), F32),
             pltpu.VMEM((2, comps, EXT, NZ), F32),
             pltpu.VMEM((2, comps, ROWS, NZ), F32),
-            pltpu.VMEM((2, 2, comps, 24, NZ), F32),
+            pltpu.VMEM((2, 9, 56, NZ), F32),
             pltpu.VMEM((2, 9, 16, NZ), F32),
-            pltpu.VMEM((2, 9, comps, 24, NZ), F32),
+            pltpu.VMEM((2, 9, 56, NZ), F32),
             pltpu.VMEM((2, 9, 16, NZ), F32),
             pltpu.VMEM((CX * CY, NZ), jnp.int32),
             pltpu.SMEM(visc_table.shape, F32),
@@ -524,7 +577,7 @@
             pltpu.VMEM(pair_gap.shape, F32),
             pltpu.VMEM(contact_force.shape, F32),
             pltpu.VMEM((PAD, 2 * NZ), F32),
-            pltpu.VMEM((SPH, ROWS, 2 * NZ), F32),
+            pltpu.VMEM((SPH, 96, 2 * NZ), F32),
             pltpu.VMEM((SPH, ROWS, NZ), F32),
             pltpu.VMEM((CHUNKS, ROWS, CHUNK), F32),
             pltpu.VMEM((CHUNKS, 2 * NZ, CHUNK), BF16),

time: 28.4 us -> 26.8 us (0.944)
  Pallas kernels: 27.6 us -> 26 us
    pallas_call x1, Pallas kernels: 26.9 us -> 25.3 us  [local(): pl.pallas_call(body, out_shape=tuple((pltpu.VMEM(shape.shape, shape.dtype...]
where the time goes in v4:
time: 26.8 us; the launch traced here: 26.6 us
  Pallas kernels  26 us (97%)
  between operations  0.64 us (2%)
    pallas_call x1, Pallas kernels, local(): pl.pallas_call(body, out_shape=tuple((pltpu.VMEM(shape.shape, shape.dtype...  25.3 us
    pallas_call x1, Pallas kernels, local(): pl.pallas_call(hand_over, out_shape=out_shape, in_specs=[vmem] * 3, out_s...  0.68 us

profile of v4, /device:TPU:31, one launch (start us, length us, event | category | flops | bytes accessed | tf_op | source)
XLA Modules:
  0.0 26.6 jit_solution(8457576950652883478)
XLA Ops:
  0.6 25.3 %shard_map.139 = (f32[3,64,128]{2,1,0:T(8,128)S(1)}, f32[3,2,2048]{2,1,0:T(2,128)S(1)}, f32[32]{0:T(128)S(1)}) custom-call(f32[3,64,128]{2,1,0:T(8,128)} %bitcast.4, f32[3,64,128]{2,1,0:T(8,128)} %bitcast.5, s32[64,128]{1,0:T(8,128)} %bitcast.6, f32[4]{0:T(128)} %table_hbm.1, f32[3,2,2048]{2,1,0:T(2,128)} %mult_hbm.1, s32[2,2048]{1,0:T(2,128)} %cell_hbm.1, ...), custom_call_target="tpu_custom_call" | custom-call | tf_op jit(solution)/shard_map/pallas_call | solution.py:549
  26.0 0.7 %shard_map.140 = (f32[3,64,128]{2,1,0:T(8,128)}, f32[3,2,2048]{2,1,0:T(2,128)}, f32[32]{0:T(128)}) custom-call(f32[3,64,128]{2,1,0:T(8,128)S(1)} %get-tuple-element.9.vel, f32[3,2,2048]{2,1,0:T(2,128)S(1)} %get-tuple-element.10.mult, f32[32]{0:T(128)S(1)} %get-tuple-element.11.contact), custom_call_target="tpu_custom_call" | custom-call | tf_op jit(solution)/shard_map/pallas_call | solution.py:602

commit v5 on v4

--- a/solution.py
+++ b/solution.py
@@ -18,8 +18,9 @@
 ROWS = 88
 PAD = 272
 EXT = 13 * 16
-HALO0, FORCE0, HALO1, FORCE1, RIGID0, RIGID1 = range(6)
+HALO0, FORCE0, HALO1, FORCE1, RIGID0, REACH = range(6)
 OTHERS = [3, 5, 0, 2, 6, 8, 1, 7]
+FAR = [(x, y) for x in range(-2, 3) for y in range(-2, 3) if (x, y) != (0, 0)]
 
 
 def row(x, y):
@@ -42,7 +43,7 @@
     own, ext, pack, halo_in, halo_diag, halo_diag_in, coef, rhs, grid, grid_pack, grid_diag, grid_in, diag_in,
     visc_class, table, cell, frac, mult, force, pair_sphere, pair_partner, normal, gap, contact,
     acc, share_acc, share, plane_w, depth_w, stack, left, mult_mid, rigid, rigid_in, normal8, contact_mid,
-    load_sem, send_sem, recv_sem,
+    spot_w, once, reach, reach_pack, reach_in, table8, table_in, load_sem, send_sem, recv_sem, far_send, far_recv,
 ):
     wide, narrow = lax.axis_index("wide"), lax.axis_index("narrow")
     n_wide, n_narrow = lax.axis_size("wide"), lax.axis_size("narrow")
@@ -73,6 +74,8 @@
     ]
     for load in loads:
         load.start()
+    ext[0:2] = jnp.zeros((2, 4, EXT, NZ), F32)
+    spot_w[...] = jnp.zeros_like(spot_w)
 
     def transfer(kind, s, src, dst):
         return pltpu.make_async_remote_copy(
@@ -111,10 +114,29 @@
             copies.append(transfer(FORCE0 if turn == 0 else FORCE1, s, src, dst))
         return copies
 
-    def rigid_copies(turn):
-        return [
-            transfer(RIGID0 if turn == 0 else RIGID1, s, rigid.at[turn], rigid_in.at[turn, s]) for s in OTHERS
-        ]
+    def rigid_copies():
+        return [transfer(RIGID0, s, rigid.at[0], rigid_in.at[s]) for s in OTHERS]
+
+    def reach_copies():
+        copies = []
+        for s in OTHERS:
+            rows = 8 if s in (0, 2, 6, 8) else 40
+            copies.append(transfer(REACH, s, reach_pack.at[8 - s, 0:rows], reach_in.at[s, 0:rows]))
+        return copies
+
+    def there(x, y):
+        return (wide + x >= 0) & (wide + x < n_wide) & (narrow + y >= 0) & (narrow + y < n_narrow)
+
+    def shift_copies():
+        copies = []
+        for x, y in FAR:
+            n = (x + 2) * 5 + y + 2
+            to = (lax.rem(wide - x + n_wide, n_wide), lax.rem(narrow - y + n_narrow, n_narrow))
+            copies.append(pltpu.make_async_remote_copy(
+                src_ref=table8, dst_ref=table_in.at[n], send_sem=far_send.at[n], recv_sem=far_recv.at[n],
+                device_id=to, device_id_type=MESH,
+            ))
+        return copies
 
     def start(copies):
         for s, copy in zip(OTHERS, copies):
@@ -425,20 +447,112 @@
 
         lax.fori_loop(1, 10, one, 0, unroll=True)
 
-    def update_contact(turn):
-        quarter = pair_q // 2
-        partner = jnp.zeros((8, 32), F32)
-        for q in range(9):
-            if q == 4:
-                tile = rigid[turn, :, 0:32]
-            else:
-                tile = received(q, rigid_in[turn, q, :, 0:32])
-            partner = jnp.where(quarter == q, tile, partner)
+    quarter = pair_q // 2
+
+    def new_contact(partner, own_tile):
         closing8 = jnp.where(sphere_row == pair_q - 2 * quarter, partner, F32(0.0)) - jnp.where(
-            sphere_row == pair_s, rigid[turn, :, 0:32], F32(0.0)
+            sphere_row == pair_s, own_tile, F32(0.0)
         )
         closing = jnp.sum(normal8[...] * closing8, axis=0, keepdims=True)
         return jnp.maximum(F32(0.0), contact_mid[...] - 0.5 * (pair_gap + closing))
+
+    def first_contact():
+        partner = jnp.zeros((8, 32), F32)
+        for q in range(9):
+            tile = rigid[0, :, 0:32] if q == 4 else received(q, rigid_in[q, :, 0:32])
+            partner = jnp.where(quarter == q, tile, partner)
+        return new_contact(partner, rigid[0, :, 0:32])
+
+    row8 = lax.broadcasted_iota(jnp.int32, (8, NZ), 0)
+    lane8 = lax.broadcasted_iota(jnp.int32, (8, NZ), 1)
+
+    def make_reach():
+        for t in range(SPH):
+            for x in range(9):
+                spot_w[t, pl.ds(row(x, 0), 8), :] = share[t, 8 + 8 * x:16 + 8 * x, :]
+            spot_w[t, pl.ds(row(0, 8), 8, stride=16), :] = share[t, 0:8, :]
+            spot_w[t, pl.ds(row(8, 8), 1), :] = share[t, 81:82, :]
+        for t in range(SPH):
+            for i in range(11):
+                to = pl.ds((i + 1) * 16, 16)
+                mid = spot_w[t, to, :]
+                value = jnp.zeros((16, NZ), F32)
+                if i < 10:
+                    value += coef[0, pl.ds((i + 1) * 16, 16), :] * spot_w[t, pl.ds((i + 2) * 16, 16), :]
+                if i > 0:
+                    value += coef[1, pl.ds((i - 1) * 16, 16), :] * spot_w[t, pl.ds(i * 16, 16), :]
+                if 0 < i < 10:
+                    at = pl.ds(i * 16, 16)
+                    value += pltpu.roll(coef[2, at, :] * mid, 15, 0) + pltpu.roll(coef[3, at, :] * mid, 1, 0)
+                    value += pltpu.roll(coef[4, at, :] * mid, NZ - 1, 1) + pltpu.roll(coef[5, at, :] * mid, 1, 1)
+                once[t, to, :] = value
+                reach[t, to, :] = coef[6, pl.ds(i * 16, 16), :] * (mid + value)
+        for s in OTHERS:
+            x = 8 if s // 3 == 2 else -1
+            y = 8 if s % 3 == 2 else -1
+            for t in range(SPH):
+                for j in range(2):
+                    if s in (1, 7):
+                        reach_pack[s, 16 * t + 8 * j:16 * t + 8 * j + 8, :] = reach[t, pl.ds(row(x + j, 0), 8), :]
+                    elif s in (3, 5):
+                        reach_pack[s, 16 * t + 8 * j:16 * t + 8 * j + 8, :] = reach[t, pl.ds(row(0, y + j), 8, stride=16), :]
+                        at = 32 + 2 * t + j
+                        reach_pack[s, at:at + 1, :] = reach[t, pl.ds(row(8, y + j), 1), :]
+                    else:
+                        at = 4 * t + 2 * j
+                        reach_pack[s, at:at + 2, :] = reach[t, pl.ds(row(x, y + j), 2, stride=16), :]
+                if s in (1, 7):
+                    reach_pack[s, 32 + 2 * t:34 + 2 * t, :] = reach[t, pl.ds(row(x, 8), 2, stride=16), :]
+
+    def column(parts):
+        tile = jnp.zeros((8, NZ), F32)
+        for (t, c), part in parts.items():
+            tile = jnp.where(row8 == 4 * t + c, jnp.sum(part, axis=0, keepdims=True), tile)
+        return jnp.sum(tile, axis=1, keepdims=True)
+
+    def given(turn):
+        table = jnp.zeros((8, NZ), F32)
+        for d in OTHERS:
+            s = 8 - d
+            parts = {}
+            for t in range(SPH):
+                for c in range(3):
+                    if d in (0, 2, 6, 8):
+                        part = reach_in[d, 4 * t:4 * t + 4, :] * grid_diag[turn, s, 4 * c:4 * c + 4, :]
+                    else:
+                        part = reach_in[d, 16 * t:16 * t + 8, :] * grid_pack[turn, s, 16 * c:16 * c + 8, :]
+                        part += reach_in[d, 16 * t + 8:16 * t + 16, :] * grid_pack[turn, s, 16 * c + 8:16 * c + 16, :]
+                        extra = reach_in[d, 32 + 2 * t:34 + 2 * t, :] * grid_pack[turn, s, 48 + 2 * c:50 + 2 * c, :]
+                        part = jnp.concatenate([part, extra], axis=0)
+                    parts[t, c] = part
+            table = jnp.where(lane8 == d, received(d, column(parts)), table)
+        return table
+
+    def kept(turn, middle, push_sum):
+        parts = {}
+        for t in range(SPH):
+            for c in range(3):
+                total = jnp.zeros((16, NZ), F32)
+                for i in range(11):
+                    at = pl.ds((i + 1) * 16, 16)
+                    total += reach[t, at, :] * rhs[turn, c, at, :] + once[t, at, :] * middle[c, at, :]
+                parts[t, c] = total
+        return column(parts) + push_sum
+
+    def last_contact():
+        lane_x, lane_y = lane8 // 3 - 1, lane8 - (lane8 // 3) * 3 - 1
+        means = table8[...]
+        for x, y in FAR + [(0, 0)]:
+            n = (x + 2) * 5 + y + 2
+            near = (lane8 < 9) & (abs(lane_x - x) <= 1) & (abs(lane_y - y) <= 1)
+            if (x, y) == (0, 0):
+                continue
+            shifted = pltpu.roll(table_in[n], (3 * x + y) % NZ, 1)
+            means += jnp.where(near & there(x, y), shifted, F32(0.0))
+        partner = jnp.zeros((8, 32), F32)
+        for q in range(9):
+            partner = jnp.where(quarter == q, means[:, q:q + 1], partner)
+        return new_contact(partner, rigid[1, :, 0:32])
 
     for turn in range(ITERS):
         last = turn == ITERS - 1
@@ -449,10 +563,20 @@
         middle, done = ext.at[2], ext.at[3]
         first_sweep(ext.at[turn], middle)
         if turn > 0:
-            arrive(rigid_copies(turn - 1))
-            contact_mid[...] = update_contact(turn - 1)
+            arrive(rigid_copies())
+            contact_mid[...] = first_contact()
         push = jnp.where(sphere_row == pair_s, normal8[...] * contact_mid[...], F32(0.0))
         push_sum = 0.5 * jnp.sum(push, axis=1, keepdims=True)
+        if last:
+            arrive(reach_copies())
+            table8[...] = jnp.where(lane8 == 4, kept(turn, middle, push_sum), given(turn))
+            for (x, y), copy in zip(FAR, shift_copies()):
+                @pl.when(there(-x, -y))
+                def go(copy=copy):
+                    copy.start()
+        else:
+            make_reach()
+            start(reach_copies())
         gather_force(turn)
         add_force(middle, turn)
         second_sweep(middle, done, turn)
@@ -469,7 +593,6 @@
             stack[c * ROWS:c * ROWS + 8, :] = done[c, pl.ds(row(0, 8), 8, stride=16), :]
             stack[c * ROWS + 81:c * ROWS + 82, :] = done[c, pl.ds(row(8, 8), 1), :]
         sums = jnp.zeros((8, NZ), F32)
-        row8 = lax.broadcasted_iota(jnp.int32, (8, NZ), 0)
         for s in range(SPH):
             for c in range(3):
                 part = jnp.sum(share[s] * stack[c * ROWS:(c + 1) * ROWS, :], axis=0, keepdims=True)
@@ -479,7 +602,7 @@
         if not last:
             pack_halo(turn + 1)
             start(halo_copies(turn + 1))
-        start(rigid_copies(turn))
+            start(rigid_copies())
         high, low = split(stack[...])
         left[0:PAD, 0:NZ] = high
         left[0:PAD, NZ:2 * NZ] = high
@@ -517,10 +640,17 @@
     for turn in range(ITERS):
         leave(halo_copies(turn))
         leave(force_copies(turn))
-    leave(rigid_copies(0))
-    arrive(rigid_copies(ITERS - 1))
-    contact_out[...] = update_contact(ITERS - 1).reshape(32)
-    leave(rigid_copies(ITERS - 1))
+    leave(rigid_copies())
+    leave(reach_copies())
+    for (x, y), copy in zip(FAR, shift_copies()):
+        @pl.when(there(-x, -y))
+        def gone(copy=copy):
+            copy.wait_send()
+
+        @pl.when(there(x, y))
+        def come(copy=copy):
+            copy.wait_recv()
+    contact_out[...] = last_contact().reshape(32)
 
 
 def hand_over(vel, mult, contact, vel_out, mult_out, contact_out, sem):
@@ -585,12 +715,21 @@
             pltpu.VMEM((2 * PAD, 2 * NZ), BF16),
             pltpu.VMEM((comps, SPH, MARK), F32),
             pltpu.VMEM((2, 8, NZ), F32),
-            pltpu.VMEM((2, 9, 8, NZ), F32),
+            pltpu.VMEM((9, 8, NZ), F32),
             pltpu.VMEM((8, 32), F32),
             pltpu.VMEM((1, 32), F32),
+            pltpu.VMEM((SPH, EXT, NZ), F32),
+            pltpu.VMEM((SPH, EXT, NZ), F32),
+            pltpu.VMEM((SPH, EXT, NZ), F32),
+            pltpu.VMEM((9, 40, NZ), F32),
+            pltpu.VMEM((9, 40, NZ), F32),
+            pltpu.VMEM((8, NZ), F32),
+            pltpu.VMEM((25, 8, NZ), F32),
             pltpu.SemaphoreType.DMA((12,)),
             pltpu.SemaphoreType.DMA((6, 9)),
             pltpu.SemaphoreType.DMA((6, 9)),
+            pltpu.SemaphoreType.DMA((25,)),
+            pltpu.SemaphoreType.DMA((25,)),
         ],
         compiler_params=pltpu.CompilerParams(
             collective_id=0, has_side_effects=True, vmem_limit_bytes=62 * 1024 * 1024

time: 26.8 us -> 25.4 us (0.948)
  Pallas kernels: 26 us -> 24.5 us
    pallas_call x1, Pallas kernels: 25.3 us -> 23.8 us  [local(): pl.pallas_call(body, out_shape=tuple((pltpu.VMEM(shape.shape, shape.dtype...]
where the time goes in v5:
time: 25.4 us; the launch traced here: 25.1 us
  Pallas kernels  24.5 us (96%)
  between operations  0.64 us (3%)
    pallas_call x1, Pallas kernels, local(): pl.pallas_call(body, out_shape=tuple((pltpu.VMEM(shape.shape, shape.dtype...  23.8 us
    pallas_call x1, Pallas kernels, local(): pl.pallas_call(hand_over, out_shape=out_shape, in_specs=[vmem] * 3, out_s...  0.68 us

profile of v5, /device:TPU:31, one launch (start us, length us, event | category | flops | bytes accessed | tf_op | source)
XLA Modules:
  0.0 25.1 jit_solution(13071761773042351160)
XLA Ops:
  0.6 23.8 %shard_map.139 = (f32[3,64,128]{2,1,0:T(8,128)S(1)}, f32[3,2,2048]{2,1,0:T(2,128)S(1)}, f32[32]{0:T(128)S(1)}) custom-call(f32[3,64,128]{2,1,0:T(8,128)} %bitcast.4, f32[3,64,128]{2,1,0:T(8,128)} %bitcast.5, s32[64,128]{1,0:T(8,128)} %bitcast.6, f32[4]{0:T(128)} %table_hbm.1, f32[3,2,2048]{2,1,0:T(2,128)} %mult_hbm.1, s32[2,2048]{1,0:T(2,128)} %cell_hbm.1, ...), custom_call_target="tpu_custom_call" | custom-call | tf_op jit(solution)/shard_map/pallas_call | solution.py:679
  24.4 0.7 %shard_map.140 = (f32[3,64,128]{2,1,0:T(8,128)}, f32[3,2,2048]{2,1,0:T(2,128)}, f32[32]{0:T(128)}) custom-call(f32[3,64,128]{2,1,0:T(8,128)S(1)} %get-tuple-element.9.vel, f32[3,2,2048]{2,1,0:T(2,128)S(1)} %get-tuple-element.10.mult, f32[32]{0:T(128)S(1)} %get-tuple-element.11.contact), custom_call_target="tpu_custom_call" | custom-call | tf_op jit(solution)/shard_map/pallas_call | solution.py:741

commit v6 on v5

--- a/solution.py
+++ b/solution.py
@@ -19,7 +19,7 @@
 PAD = 272
 EXT = 13 * 16
 HALO0, FORCE0, HALO1, FORCE1, RIGID0, REACH = range(6)
-OTHERS = [3, 5, 0, 2, 6, 8, 1, 7]
+OTHERS = [0, 2, 6, 8, 3, 5, 1, 7]
 FAR = [(x, y) for x in range(-2, 3) for y in range(-2, 3) if (x, y) != (0, 0)]
 
 
@@ -56,6 +56,17 @@
         dx, dy = d // 3 - 1, d % 3 - 1
         return (wide + dx >= 0) & (wide + dx < n_wide) & (narrow + dy >= 0) & (narrow + dy < n_narrow)
 
+    loads = [
+        pltpu.make_async_copy(src, dst, load_sem.at[k])
+        for k, (src, dst) in enumerate((
+            (cell_hbm, cell), (frac_hbm, frac), (mult_hbm, mult), (class_hbm, visc_class), (table_hbm, table),
+            (vel_hbm, own.at[0, 0:3]), (force_hbm, force), (sphere_hbm, pair_sphere), (partner_hbm, pair_partner),
+            (normal_hbm, normal), (gap_hbm, gap), (contact_hbm, contact),
+        ))
+    ]
+    for load in loads:
+        load.start()
+
     barrier = pltpu.get_barrier_semaphore()
     for d in OTHERS:
         @pl.when(exists(d))
@@ -64,16 +75,6 @@
     across = jnp.where(wide > 0, 1, 0) + jnp.where(wide < n_wide - 1, 1, 0) + 1
     along = jnp.where(narrow > 0, 1, 0) + jnp.where(narrow < n_narrow - 1, 1, 0) + 1
 
-    loads = [
-        pltpu.make_async_copy(src, dst, load_sem.at[k])
-        for k, (src, dst) in enumerate((
-            (class_hbm, visc_class), (table_hbm, table), (vel_hbm, own.at[0, 0:3]), (cell_hbm, cell), (frac_hbm, frac),
-            (mult_hbm, mult), (force_hbm, force), (sphere_hbm, pair_sphere), (partner_hbm, pair_partner),
-            (normal_hbm, normal), (gap_hbm, gap), (contact_hbm, contact),
-        ))
-    ]
-    for load in loads:
-        load.start()
     ext[0:2] = jnp.zeros((2, 4, EXT, NZ), F32)
     spot_w[...] = jnp.zeros_like(spot_w)
 
@@ -195,7 +196,7 @@
                         s, halo_diag_in[turn, s, at:at + len(xs), :]
                     )
 
-    for load in loads[0:3]:
+    for load in loads[3:6]:
         load.wait()
     classes = visc_class[...]
     mu = jnp.where(classes == 0, table[0], jnp.where(classes == 1, table[1], jnp.where(classes == 2, table[2], table[3])))
@@ -206,7 +207,7 @@
             ext[0, f, pl.ds(row(x, 0), 8), :] = own[0, f, 8 * x:8 * x + 8, :]
     pack_halo(0)
 
-    for load in loads[3:]:
+    for load in loads[0:3] + loads[6:]:
         load.wait()
     acc[...] = jnp.zeros_like(acc)
     share_acc[...] = jnp.zeros_like(share_acc)
@@ -214,9 +215,9 @@
     def add_spread(lhs, depth):
         high, low = split(lhs)
         dims = (((1,), (1,)), ((), ()))
-        return lax.dot_general(high, depth, dims, preferred_element_type=F32) + lax.dot_general(
-            low, depth, dims, preferred_element_type=F32
-        )
+        both = lax.dot_general(high, depth, dims, preferred_element_type=F32)
+        rest = lax.dot_general(low, depth[0:NZ], dims, preferred_element_type=F32)
+        return both[:, 0:NZ] + both[:, NZ:2 * NZ] + rest
 
     def setup(n, carry):
         s, k = n // PER_SPHERE, n % PER_SPHERE
@@ -264,7 +265,7 @@
         for c in range(3):
             base = c * ROWS
             for t in range(11):
-                part = acc[base + 8 * t:base + 8 * t + 8, 0:NZ] + acc[base + 8 * t:base + 8 * t + 8, NZ:2 * NZ]
+                part = acc[base + 8 * t:base + 8 * t + 8, :]
                 if 1 <= t <= 8:
                     part = part + force[c, 8 * t - 8:8 * t, :]
                 grid[turn, c, 8 * t:8 * t + 8, :] = part
@@ -307,9 +308,9 @@
 
     lax.fori_loop(0, PER_SPHERE, shares, 0, unroll=4)
     for s in range(SPH):
-        share[s] = (share_acc[s, 0:ROWS, 0:NZ] + share_acc[s, 0:ROWS, NZ:2 * NZ]) * F32(1.0 / MARK)
-
-    rhs[...] = jnp.zeros_like(rhs)
+        share[s] = share_acc[s, 0:ROWS, :] * F32(1.0 / MARK)
+
+    rhs[0:2] = jnp.zeros((2, 3, EXT, NZ), F32)
     stack[...] = jnp.zeros_like(stack)
     normal8[...] = jnp.zeros_like(normal8)
     normal8[0:3, :] = normal[...]
@@ -528,7 +529,7 @@
             table = jnp.where(lane8 == d, received(d, column(parts)), table)
         return table
 
-    def kept(turn, middle, push_sum):
+    def kept(turn, middle):
         parts = {}
         for t in range(SPH):
             for c in range(3):
@@ -537,7 +538,7 @@
                     at = pl.ds((i + 1) * 16, 16)
                     total += reach[t, at, :] * rhs[turn, c, at, :] + once[t, at, :] * middle[c, at, :]
                 parts[t, c] = total
-        return column(parts) + push_sum
+        return column(parts)
 
     def last_contact():
         lane_x, lane_y = lane8 // 3 - 1, lane8 - (lane8 // 3) * 3 - 1
@@ -563,17 +564,22 @@
         middle, done = ext.at[2], ext.at[3]
         first_sweep(ext.at[turn], middle)
         if turn > 0:
+            mean_kept = kept(turn, middle)
             arrive(rigid_copies())
             contact_mid[...] = first_contact()
         push = jnp.where(sphere_row == pair_s, normal8[...] * contact_mid[...], F32(0.0))
         push_sum = 0.5 * jnp.sum(push, axis=1, keepdims=True)
         if last:
-            arrive(reach_copies())
-            table8[...] = jnp.where(lane8 == 4, kept(turn, middle, push_sum), given(turn))
+            table8[...] = jnp.where(lane8 == 4, mean_kept + push_sum, table8[...])
             for (x, y), copy in zip(FAR, shift_copies()):
                 @pl.when(there(-x, -y))
                 def go(copy=copy):
                     copy.start()
+            for turn_before in range(ITERS):
+                leave(halo_copies(turn_before))
+            leave(force_copies(0))
+            leave(rigid_copies())
+            leave(reach_copies())
         else:
             make_reach()
             start(reach_copies())
@@ -616,7 +622,7 @@
             s, k = n // PER_SPHERE, n % PER_SPHERE
             lanes = pl.ds(pl.multiple_of(k * CHUNK, CHUNK), CHUNK)
             weight = plane_w[n]
-            sampled = jnp.dot(left[0:PAD], depth_w[n], preferred_element_type=F32) + jnp.dot(left[PAD:2 * PAD], depth_w[n], preferred_element_type=F32)
+            sampled = jnp.dot(left[0:PAD], depth_w[n], preferred_element_type=F32) + jnp.dot(left[PAD:2 * PAD, 0:NZ], depth_w[n, 0:NZ], preferred_element_type=F32)
             lhs = []
             for c in range(3):
                 rows = slice(c * ROWS, (c + 1) * ROWS)
@@ -637,19 +643,17 @@
         lax.fori_loop(0, CHUNKS, markers, 0, unroll=8)
         if not last:
             send_force(turn + 1)
-    for turn in range(ITERS):
-        leave(halo_copies(turn))
-        leave(force_copies(turn))
-    leave(rigid_copies())
-    leave(reach_copies())
+            arrive(reach_copies())
+            table8[...] = given(turn + 1)
+    leave(force_copies(ITERS - 1))
     for (x, y), copy in zip(FAR, shift_copies()):
+        @pl.when(there(x, y))
+        def come(copy=copy):
+            copy.wait_recv()
+
         @pl.when(there(-x, -y))
         def gone(copy=copy):
             copy.wait_send()
-
-        @pl.when(there(x, y))
-        def come(copy=copy):
-            copy.wait_recv()
     contact_out[...] = last_contact().reshape(32)
 
 
@@ -689,8 +693,8 @@
             pltpu.VMEM((2, 9, 40, NZ), F32),
             pltpu.VMEM((2, 9, 40, NZ), F32),
             pltpu.VMEM((7, 11 * 16, NZ), F32),
-            pltpu.VMEM((2, comps, EXT, NZ), F32),
-            pltpu.VMEM((2, comps, ROWS, NZ), F32),
+            pltpu.VMEM((3, comps, EXT, NZ), F32),
+            pltpu.VMEM((3, comps, ROWS, NZ), F32),
             pltpu.VMEM((2, 9, 56, NZ), F32),
             pltpu.VMEM((2, 9, 16, NZ), F32),
             pltpu.VMEM((2, 9, 56, NZ), F32),
@@ -706,8 +710,8 @@
             pltpu.VMEM(pair_normal.shape, F32),
             pltpu.VMEM(pair_gap.shape, F32),
             pltpu.VMEM(contact_force.shape, F32),
-            pltpu.VMEM((PAD, 2 * NZ), F32),
-            pltpu.VMEM((SPH, 96, 2 * NZ), F32),
+            pltpu.VMEM((PAD, NZ), F32),
+            pltpu.VMEM((SPH, 96, NZ), F32),
             pltpu.VMEM((SPH, ROWS, NZ), F32),
             pltpu.VMEM((CHUNKS, ROWS, CHUNK), F32),
             pltpu.VMEM((CHUNKS, 2 * NZ, CHUNK), BF16),
@@ -720,7 +724,7 @@
             pltpu.VMEM((1, 32), F32),
             pltpu.VMEM((SPH, EXT, NZ), F32),
             pltpu.VMEM((SPH, EXT, NZ), F32),
-            pltpu.VMEM((SPH, EXT, NZ), F32),
+            pltpu.VMEM((SPH + 1, EXT, NZ), F32),
             pltpu.VMEM((9, 40, NZ), F32),
             pltpu.VMEM((9, 40, NZ), F32),
             pltpu.VMEM((8, NZ), F32),

time: 25.4 us -> 25.1 us (0.988)
  the two profiles are of different devices: /device:TPU:31 before, /device:TPU:22 now
where the time goes in v6:
time: 25.1 us; the launch traced here: 24.9 us
  Pallas kernels  24.3 us (97%)
  between operations  0.64 us (3%)
    pallas_call x1, Pallas kernels, local(): pl.pallas_call(body, out_shape=tuple((pltpu.VMEM(shape.shape, shape.dtype...  23.6 us
    pallas_call x1, Pallas kernels, local(): pl.pallas_call(hand_over, out_shape=out_shape, in_specs=[vmem] * 3, out_s...  0.68 us

profile of v6, /device:TPU:22, one launch (start us, length us, event | category | flops | bytes accessed | tf_op | source)
XLA Modules:
  0.0 24.9 jit_solution(8999130736042350726)
XLA Ops:
  0.6 23.6 %shard_map.139 = (f32[3,64,128]{2,1,0:T(8,128)S(1)}, f32[3,2,2048]{2,1,0:T(2,128)S(1)}, f32[32]{0:T(128)S(1)}) custom-call(f32[3,64,128]{2,1,0:T(8,128)} %bitcast.4, f32[3,64,128]{2,1,0:T(8,128)} %bitcast.5, s32[64,128]{1,0:T(8,128)} %bitcast.6, f32[4]{0:T(128)} %table_hbm.1, f32[3,2,2048]{2,1,0:T(2,128)} %mult_hbm.1, s32[2,2048]{1,0:T(2,128)} %cell_hbm.1, ...), custom_call_target="tpu_custom_call" | custom-call | tf_op jit(solution)/shard_map/pallas_call | solution.py:683
  24.3 0.7 %shard_map.140 = (f32[3,64,128]{2,1,0:T(8,128)}, f32[3,2,2048]{2,1,0:T(2,128)}, f32[32]{0:T(128)}) custom-call(f32[3,64,128]{2,1,0:T(8,128)S(1)} %get-tuple-element.9.vel, f32[3,2,2048]{2,1,0:T(2,128)S(1)} %get-tuple-element.10.mult, f32[32]{0:T(128)S(1)} %get-tuple-element.11.contact), custom_call_target="tpu_custom_call" | custom-call | tf_op jit(solution)/shard_map/pallas_call | solution.py:745
